TPU v7x, 32 devices: a whole 2x2x4 slice. The times are simulated.
32 devices in a mesh: groups: 4 (over y, core), shards: 2 (over x), tensor: 4 (over z).
Axes of the slice: x: 2, y: 2, z: 4, core: 2. Of those that a mesh axis runs over, the one named last changes fastest.
Arguments:
- global_layer: float32 [3, 2816, 1024], P(None, 'tensor', 'shards'), may hold values from -6 to 6
- local_layer: bfloat16 [4, 3, 2816, 1024], P('groups', None, 'tensor', 'shards'), may hold values from -6 to 6
- layer_momentum: float32 [3, 2816, 1024], P(None, 'tensor', 'shards'), may hold values from -6 to 6
- global_embed: float32 [32000, 1024], P('shards', 'tensor'), may hold values from -6 to 6
- local_embed: bfloat16 [4, 32000, 1024], P('groups', 'shards', 'tensor'), may hold values from -6 to 6
- embed_momentum: float32 [32000, 1024], P('shards', 'tensor'), may hold values from -6 to 6
- projection: float32 [1024, 64], P('tensor'), may hold values from -0.1875 to 0.1875
Outputs:
- new_layer: float32 [3, 2816, 1024], P(None, 'tensor', 'shards')
- new_layer_momentum: float32 [3, 2816, 1024], P(None, 'tensor', 'shards')
- new_embed: float32 [32000, 1024], P('shards', 'tensor')
- new_embed_momentum: float32 [32000, 1024], P('shards', 'tensor')
All inputs are finite; a program needn't handle non-finite values.
Results may differ from a plain program's by a relative error of at most 0.0003.
Values sent between devices are 32-bit elements; how exact they have to be, the bound alone decides.
No kernel may reach another device: no remote copies, remote signals or barrier semaphores. Data moves between devices by JAX's collectives and lax.ppermute only.
A program may use at most 192 MiB of HBM per device.

v0:
```python
import jax
import jax.numpy as jnp
from jax import lax
from jax.sharding import PartitionSpec as P

momentum_rate = 0.9
outer_rate = 0.7


def nesterov(weights, momentum, delta):
    moved = momentum_rate * momentum + delta
    return (weights - outer_rate * (delta + momentum_rate * moved), moved)


def body(
    global_layer, local_layer, layer_momentum, global_embed, local_embed, embed_momentum, projection
):
    group_count = lax.axis_size("groups")
    difference = global_embed - local_embed[0].astype(jnp.float32)
    partial_proj = jnp.dot(
        difference, projection, precision=lax.Precision.HIGHEST, preferred_element_type=jnp.float32
    )
    layer_terms = global_layer - local_layer[0].astype(jnp.float32)
    projected = lax.psum(partial_proj, ("groups", "tensor"))
    projected = projected / group_count
    summed = lax.psum(layer_terms, "groups")
    layer_delta = summed / group_count
    new_layer, new_layer_momentum = nesterov(global_layer, layer_momentum, layer_delta)
    embed_delta = jnp.dot(
        projected, projection.T, precision=lax.Precision.HIGHEST, preferred_element_type=jnp.float32
    )
    new_embed, new_embed_momentum = nesterov(global_embed, embed_momentum, embed_delta)
    return (new_layer, new_layer_momentum, new_embed, new_embed_momentum)


def solution(mesh):
    in_specs = (
        P(None, "tensor", "shards"),
        P("groups", None, "tensor", "shards"),
        P(None, "tensor", "shards"),
        P("shards", "tensor"),
        P("groups", "shards", "tensor"),
        P("shards", "tensor"),
        P("tensor", None),
    )
    out_specs = (
        P(None, "tensor", "shards"),
        P(None, "tensor", "shards"),
        P("shards", "tensor"),
        P("shards", "tensor"),
    )
    return jax.shard_map(body, mesh=mesh, in_specs=in_specs, out_specs=out_specs, check_vma=False)
```

profile of v0, /device:TPU:0, one launch (start us, length us, event | category | flops | bytes accessed | tf_op | source)
XLA Modules:
  0.0 250.7 jit_solution(9109371655628692409)
XLA Ops:
  7.2 0.0 copy-start
  7.2 0.0 all-reduce.5.cloned.1.call-start
  7.2 0.8 copy-done
  8.0 22.1 %fusion = f32[16000,64]{0,1:T(8,128)} fusion(f32[256,64]{0,1:T(8,128)S(1)} %copy-done, f32[16000,256]{1,0:T(8,128)} %param.10, bf16[1,16000,256]{2,1,0:T(8,128)(2,1)} %param.11), kind=kOutput, calls=%fused_computation.1 | convolution fusion | flops 3153920000 | bytes 28737536 | tf_op jit(solution)/shard_map/dot_general | solution.py:20
  30.1 0.0 copy-start.2
  30.1 0.0 all-reduce.5.cloned.1.call-update
  30.2 0.2 all-reduce.3.cloned.1.call-start
  30.4 1.4 copy-done.2
  31.8 5.1 %convert_subtract_fusion.2 = f32[3,704,512]{2,1,0:T(8,128)} fusion(f32[3,704,512]{2,1,0:T(8,128)} %param.7, bf16[1,3,704,512]{3,2,1,0:T(8,128)(2,1)S(1)} %copy-done.2), kind=kLoop, calls=%fused_computation.5 | loop fusion | flops 2162688 | bytes 10813440 | tf_op jit(solution)/shard_map/sub | solution.py:23
  36.9 0.0 all-reduce.3.cloned.1.call-update
  36.9 106.6 %all-reduce.5.cloned.1.call-done = f32[16000,64]{0,1:T(8,128)} async-done(((f32[16000,64]{0,1:T(8,128)}), f32[16000,64]{0,1:T(8,128)}) %all-reduce.5.cloned.1.call-update) | async-done | bytes 4096016 | tf_op jit(solution)/shard_map/psum | solution.py:24
  143.5 31.9 %multiply_subtract_fusion = (f32[16000,256]{1,0:T(8,128)}, f32[16000,256]{1,0:T(8,128)}) fusion(f32[16000,256]{1,0:T(8,128)} %param.10, f32[16000,256]{1,0:T(8,128)} %param.12, f32[256,64]{0,1:T(8,128)S(1)} %copy-done, f32[16000,64]{0,1:T(8,128)} %all-reduce.5.cloned.1.call-done), kind=kOutput, calls=%fused_computation.2 | convolution fusion | flops 3171328000 | bytes 69697536 | tf_op jit(solution)/shard_map/dot_general | solution.py:29
  175.4 57.9 %all-reduce.3.cloned.1.call-done = f32[3,704,512]{2,1,0:T(8,128)} async-done(((f32[3,704,512]{2,1,0:T(8,128)}), f32[3,704,512]{2,1,0:T(8,128)}) %all-reduce.3.cloned.1.call-update) | async-done | bytes 4325392 | tf_op jit(solution)/shard_map/psum | solution.py:26
  233.3 0.0 copy-start.1
  233.3 10.5 %multiply_subtract_fusion.1 = (f32[3,704,512]{2,1,0:T(8,128)}, f32[3,704,512]{2,1,0:T(8,128)}) fusion(f32[3,704,512]{2,1,0:T(8,128)} %param.7, f32[3,704,512]{2,1,0:T(8,128)} %all-reduce.3.cloned.1.call-done, f32[3,704,512]{2,1,0:T(8,128)} %param.9), kind=kLoop, calls=%fused_computation.6 | loop fusion | flops 7569408 | bytes 21626880 | tf_op jit(solution)/shard_map/sub | solution.py:12
  243.8 0.0 copy-done.1
Async XLA Ops:
  7.2 0.8 copy-start
  7.2 136.3 %all-reduce.5.cloned.1.call-start = ((), (), s32[]{:S(2)}) async-start(), calls=%async_computation.1 | async-start | bytes 8192000 | tf_op jit(solution)/shard_map/psum | solution.py:24
  30.1 1.6 copy-start.2
  30.2 203.1 %all-reduce.3.cloned.1.call-start = ((), (), s32[]{:S(2)}) async-start(), calls=%async_computation | async-start | bytes 8650752 | tf_op jit(solution)/shard_map/psum | solution.py:26
  233.3 10.6 %copy-start.1 = (f32[256,64]{0,1:T(8,128)S(1)}, f32[256,64]{0,1:T(8,128)}, u32[]{:S(2)}) copy-start(f32[256,64]{0,1:T(8,128)} %param.13) | copy-start | bytes 196612
Sparse Core Ops, SparseCore 0:
  30.3 113.1 all-reduce.4
  146.6 86.6 all-reduce.2
where the time goes:
time: 251 us
  waiting for transfers between devices  165 us (66%)
  matrix products  54 us (22%)
  other arithmetic  15.7 us (6%)
  between operations  14 us (6%)
    psum x1, waiting for transfers between devices, body(): projected = lax.psum(partial_proj, ('groups', 'tensor'))  107 us
    psum x1, waiting for transfers between devices, body(): summed = lax.psum(layer_terms, 'groups')  57.9 us
    dot_general x1, matrix products, body(): jnp.dot(projected, projection.T, precision=lax.Precision.HIGHEST, preferr...  31.9 us
    dot_general x1, matrix products, body(): jnp.dot(difference, projection, precision=lax.Precision.HIGHEST, preferre...  22.1 us
    sub x1, other arithmetic, nesterov(): return (weights - outer_rate * (delta + momentum_rate * moved), moved)  10.5 us
    sub x1, other arithmetic, body(): layer_terms = global_layer - local_layer[0].astype(jnp.float32)  5.12 us
  transfers between devices with their start and end apart: 2, of which 2 were waited for; matrix products, arithmetic and copies ran while one was open for 15% of the time, Pallas kernels for 0%

commit v1 on v0

v1 whole, which is shorter than its diff:
```python
import functools

import jax
import jax.numpy as jnp
import numpy as np
from jax import lax
from jax.experimental import pallas as pl
from jax.experimental.pallas import tpu as pltpu
from jax.sharding import PartitionSpec as P

momentum_rate = 0.9
outer_rate = 0.7
GRAIN = 16
UNIT = 176
COST = pl.CostEstimate(flops=0, bytes_accessed=0, transcendentals=0)
PARAMS = pltpu.CompilerParams(vmem_limit_bytes=53 * 1024 * 1024)


def nesterov(weights, momentum, delta):
    moved = momentum_rate * momentum + delta
    return (weights - outer_rate * (delta + momentum_rate * moved), moved)


def halves(value):
    high = value.astype(jnp.bfloat16)
    return high, (value - high.astype(jnp.float32)).astype(jnp.bfloat16)


def dot(a, b):
    return jnp.dot(a, b, preferred_element_type=jnp.float32)


class Table:
    def __init__(self, groups, tensor):
        self.shape = (groups, tensor)
        self.columns = []
        self.size = 0

    def add(self, entry):
        block = np.array([[entry(g, z) for z in range(self.shape[1])] for g in range(self.shape[0])], np.int32)
        at = self.size
        self.columns.append(block)
        self.size += block.shape[2]
        return at

    def mine(self):
        whole = jnp.asarray(np.concatenate(self.columns, axis=2))
        row = lax.dynamic_slice(
            whole, (lax.axis_index("groups"), lax.axis_index("tensor"), 0), (1, 1, self.size)
        )
        return row.reshape(self.size)


HBM = pl.BlockSpec(memory_space=pltpu.HBM)
VMEM = pl.BlockSpec(memory_space=pltpu.VMEM)
SMEM = pl.BlockSpec(memory_space=pltpu.SMEM)
ANY = pl.BlockSpec(memory_space=pl.ANY)


def rows_at(ref, place, unit, offset, size):
    return ref.at[pl.ds(pl.multiple_of(place * unit + offset, 8), size)]


def project_kernel(at, count, tile, tab, g, l, p, *refs):
    out, g_in, l_in, p_in, w, sem, p_sem = refs[-7:]
    rank, width = p.shape
    half = tile // 2
    fetch = pltpu.make_async_copy(p, p_in, p_sem)
    fetch.start()
    copies = []
    for i in range(count):
        pair = [
            pltpu.make_async_copy(rows_at(x, tab[at + i], GRAIN, 0, tile), to.at[i], sem.at[n, i])
            for n, (x, to) in enumerate(((g, g_in), (l, l_in)))
        ]
        for copy in pair:
            copy.start()
        copies.append(pair)
    if len(refs) > 7:
        add = pltpu.make_async_copy(refs[0], out, p_sem)
    fetch.wait()
    if len(refs) > 7:
        add.start()
    high, low = (x.T for x in halves(p_in[...]))
    none = jnp.zeros_like(high)
    w[0:width] = jnp.concatenate([high, none, low, none], axis=1)
    w[width:] = jnp.concatenate([none, high, none, low], axis=1)
    if len(refs) > 7:
        add.wait()
    for i in range(count):
        for copy in copies[i]:
            copy.wait()
        difference = g_in[i] - l_in[i].astype(jnp.float32)
        high, low = halves(jnp.concatenate([difference[:half], difference[half:]], axis=1))
        wide = dot(high, w[...])
        mine = wide[:, 0 : 2 * rank] + wide[:, 2 * rank :] + dot(low, w[:, 0 : 2 * rank])
        rows = slice(i * half, (i + 1) * half)
        out[rows] = mine + out[rows] if len(refs) > 7 else mine


def project(tab, at, count, tile, global_embed, local_embed, projection_t, *got):
    width = global_embed.shape[1]
    rank = projection_t.shape[0]
    return pl.pallas_call(
        functools.partial(project_kernel, at, count, tile),
        in_specs=[SMEM, HBM, HBM, HBM] + [ANY] * len(got),
        out_specs=VMEM,
        out_shape=jax.ShapeDtypeStruct((count * tile // 2, 2 * rank), jnp.float32),
        scratch_shapes=[
            pltpu.VMEM((count, tile, width), jnp.float32),
            pltpu.VMEM((count, tile, width), jnp.bfloat16),
            pltpu.VMEM((rank, width), jnp.float32),
            pltpu.VMEM((2 * width, 4 * rank), jnp.bfloat16),
            pltpu.SemaphoreType.DMA((2, count)),
            pltpu.SemaphoreType.DMA(()),
        ],
        compiler_params=PARAMS,
        cost_estimate=COST,
        name="project",
    )(tab, global_embed, local_embed, projection_t, *got)


def update_kernel(at, unit, sub, subs, depth, parts, delta_of, extra, fixed, scratch, tab, *refs):
    far, (g, m) = refs[:extra], refs[extra : extra + 2]
    refs, scratch = refs[: len(refs) - scratch - fixed], refs[len(refs) - scratch - fixed :]
    new_g, new_m, g_in, m_in, g_out, m_out, packed, sem, source_sem, constant_sem = refs[-10:]
    near, scratch = scratch[:fixed], scratch[fixed:]
    count = parts

    def incoming(i, j):
        place, n = tab[at + count + i], i * subs + j
        return [
            pltpu.make_async_copy(rows_at(x, place, unit, j * sub, sub), to.at[n], sem.at[k, n])
            for k, (x, to) in enumerate(((g, g_in), (m, m_in)))
        ]

    def outgoing(i, j):
        place, n = tab[at + count + i], i * subs + j
        return [
            pltpu.make_async_copy(x.at[n], rows_at(to, place, unit, j * sub, sub), sem.at[2 + k, n])
            for k, (x, to) in enumerate(((g_out, new_g), (m_out, new_m)))
        ]

    def when_there(i, step):
        pl.when(tab[at + i] == 1)(step)

    def brought(i, source):
        here = pl.ds(pl.multiple_of(tab[at + 3 * count + i] * depth, 8), depth)
        return pltpu.make_async_copy(far[source].at[here], packed.at[i], source_sem.at[i])

    constant = [pltpu.make_async_copy(x, to, constant_sem) for x, to in zip(far[extra - fixed :], near)]
    for copy in constant:
        copy.start()
    for i in range(count):

        @functools.partial(when_there, i)
        def _(i=i):
            for n in range(extra - fixed):

                @pl.when(tab[at + 2 * count + i] == n)
                def _(n=n):
                    brought(i, n).start()

            for j in range(subs):
                for copy in incoming(i, j):
                    copy.start()

    for copy in constant:
        copy.wait()
    delta = delta_of(scratch, near)
    for i in range(count):

        @functools.partial(when_there, i)
        def _(i=i):
            brought(i, 0).wait()
            change = delta(packed.at[i])
            for j in range(subs):
                n = i * subs + j
                for copy in incoming(i, j):
                    copy.wait()
                weights = g_in[n]
                g_out[n], m_out[n] = nesterov(weights, m_in[n], change(j, weights))
                for copy in outgoing(i, j):
                    copy.start()

    for i in range(count):

        @functools.partial(when_there, i)
        def _(i=i):
            for j in range(subs):
                for copy in outgoing(i, j):
                    copy.wait()


def update(
    tab, at, unit, sub, subs, depth, parts, delta_of, sources, constants, weights, momentum, before, scratch, name
):
    rows, width = weights.shape
    extra = [] if before is None else list(before)
    count = parts * subs
    inputs = [*sources, *constants]
    where = 3 + len(inputs)
    return pl.pallas_call(
        functools.partial(
            update_kernel, at, unit, sub, subs, depth, parts, delta_of, len(inputs), len(constants), len(scratch)
        ),
        in_specs=[SMEM] + [ANY] * len(inputs) + [HBM] * (2 + len(extra)),
        out_specs=[HBM, HBM],
        out_shape=[jax.ShapeDtypeStruct((rows, width), jnp.float32)] * 2,
        input_output_aliases={} if before is None else {where: 0, where + 1: 1},
        scratch_shapes=[pltpu.VMEM((count, sub, width), jnp.float32)] * 4
        + [pltpu.VMEM((parts, depth, sources[0].shape[1]), jnp.float32)]
        + [pltpu.SemaphoreType.DMA((4, count)), pltpu.SemaphoreType.DMA((parts,)), pltpu.SemaphoreType.DMA(())]
        + [pltpu.VMEM(x.shape, x.dtype) for x in constants]
        + scratch,
        compiler_params=PARAMS,
        cost_estimate=COST,
        name=name,
    )(tab, *inputs, weights, momentum, *extra)


def embed_update(tab, at, tile, parts, sources, projection_t, weights, momentum, groups, before):
    width = weights.shape[1]
    rank = projection_t.shape[0]
    half = tile // 2

    def delta_of(scratch, refs):
        (w,) = scratch
        high, low = halves(refs[0][...])
        w[...] = jnp.zeros_like(w)
        for j in range(2):
            w[j, j * rank : (j + 1) * rank] = high
            w[j, (2 + j) * rank : (3 + j) * rank] = high
            w[j, (4 + j) * rank : (5 + j) * rank] = low

        def delta(packed):
            high, low = halves(packed[...] * (1 / groups))
            parts = jnp.concatenate([high, low, high], axis=1)
            return lambda j, weights: dot(parts, w[j])

        return delta

    scratch = [pltpu.VMEM((2, 6 * rank, width), jnp.bfloat16)]
    return update(
        tab, at, GRAIN, half, 2, half, parts, delta_of, sources, [projection_t], weights, momentum, before, scratch,
        "embed_update",
    )


def layer_update(tab, at, parts, sources, weights, momentum, groups, before):
    def delta_of(scratch, refs):
        return lambda packed: lambda j, weights: weights - packed[...] * (1 / groups)

    return update(
        tab, at, UNIT, UNIT, 1, UNIT, parts, delta_of, sources, [], weights, momentum, before, [], "layer_update"
    )


def widen_kernel(at, sizes, added, tab, l, *refs):
    got, outs, (l_in, sem), near = refs[:added], refs[added : -2 - added], refs[-2 - added :][:2], refs[len(refs) - added :]
    copies = [pltpu.make_async_copy(rows_at(l, tab[at], UNIT, 0, sum(sizes)), l_in, sem.at[0])]
    copies += [pltpu.make_async_copy(x, to, sem.at[1]) for x, to in zip(got, near)]
    for copy in copies:
        copy.start()
    for copy in copies:
        copy.wait()
    first = 0
    for out, size in zip(outs, sizes):
        value = l_in[first : first + size].astype(jnp.float32)
        out[...] = value + near[0][first : first + size] if added else value
        first += size


def widen(tab, at, sizes, local, *got):
    width = local.shape[1]
    return pl.pallas_call(
        functools.partial(widen_kernel, at, sizes, len(got)),
        in_specs=[SMEM, HBM] + [ANY] * len(got),
        out_specs=[VMEM] * len(sizes),
        out_shape=[jax.ShapeDtypeStruct((size, width), jnp.float32) for size in sizes],
        scratch_shapes=[pltpu.VMEM((sum(sizes), width), jnp.bfloat16), pltpu.SemaphoreType.DMA((2,))]
        + [pltpu.VMEM(x.shape, x.dtype) for x in got],
        compiler_params=PARAMS,
        cost_estimate=COST,
        name="widen",
    )(tab, local, *got)


class Order:
    def __init__(self):
        self.last = None

    def after(self, x):
        if self.last is None:
            return x
        return lax.optimization_barrier((x, self.last))[0]

    def done(self, x):
        self.last = x[0] if isinstance(x, (list, tuple)) else x
        return x


def swap_groups(x, bit):
    return lax.ppermute(x, "groups", [(g, g ^ bit) for g in range(4)])


def shift(x, step):
    pairs = []
    for g in range(4):
        for z in range(4):
            to = z + 1 if g % 2 == 0 else z - 1
            first = z if g % 2 == 0 else 3 - z
            if 0 <= to < 4 and first >= step:
                pairs.append((g * 4 + z, g * 4 + to))
    return lax.ppermute(x, ("groups", "tensor"), pairs)


def plain(
    global_layer, local_layer, layer_momentum, global_embed, local_embed, embed_momentum, projection
):
    groups = lax.axis_size("groups")
    exact = {"precision": lax.Precision.HIGHEST, "preferred_element_type": jnp.float32}
    projected = jnp.dot(global_embed - local_embed[0].astype(jnp.float32), projection, **exact)
    projected = lax.psum(projected, ("groups", "tensor")) / groups
    layer_delta = lax.psum(global_layer - local_layer[0].astype(jnp.float32), "groups") / groups
    embed_delta = jnp.dot(projected, projection.T, **exact)
    return (
        *nesterov(global_layer, layer_momentum, layer_delta),
        *nesterov(global_embed, embed_momentum, embed_delta),
    )


def body(
    global_layer, local_layer, layer_momentum, global_embed, local_embed, embed_momentum, projection
):
    groups = lax.axis_size("groups")
    tensor = lax.axis_size("tensor")
    rows, width = global_embed.shape
    weights = global_layer.reshape(-1, global_layer.shape[-1])
    units = weights.shape[0] // UNIT // 2
    grains = rows // (8 * GRAIN)
    whole = rows % (8 * GRAIN) == 0 and 8 <= grains <= 125 and weights.shape[0] % (2 * UNIT) == 0 and units == 6
    if not whole or (groups, tensor) != (4, 4) or width % 256 or projection.shape[1] != 64:
        return plain(
            global_layer, local_layer, layer_momentum, global_embed, local_embed, embed_momentum, projection
        )
    projection_t = projection.T
    embed_local = local_embed[0]
    momentum = layer_momentum.reshape(weights.shape)
    local = local_layer[0].reshape(weights.shape)
    table = Table(groups, tensor)
    chunks = [grains * 14 // 25]
    chunks.append(grains - sum(chunks))
    tiles = [n * GRAIN for n in chunks]
    bases = [0, 8 * chunks[0]]

    def core(g):
        return g % 2

    def place(c, h, k):
        return bases[c] + (h * 4 + k) * chunks[c]

    p_send = [table.add(lambda g, z, c=c: [place(c, 1 - core(g), k) for k in range(4)]) for c in range(2)]
    p_keep = [table.add(lambda g, z, c=c: [place(c, core(g), k) for k in range(4)]) for c in range(2)]

    def blocks_at(c, first):
        def entry(g, z):
            blocks = []
            for n in range(4):
                for h, k in ((core(g), z - n), (1 - core(g), z + n)):
                    k = 2 * z - k if core(g) else k
                    if n or h == core(g):
                        blocks.append((len(blocks), h, k))
            beside = [b for b in blocks[1:3] if 0 <= b[2] < 4][0]
            early = [blocks[0], beside]
            turn = early if first else [b for b in blocks if b not in early and 0 <= b[2] < 4]
            parts = [(place(c, h ^ half, k), n if first else n - 1, half) for n, h, k in turn for half in (0, 1)]
            return [1] * len(parts) + [p for column in zip(*parts) for p in column]

        return table.add(entry)

    near = [blocks_at(c, True) for c in range(2)]
    far = [blocks_at(c, False) for c in range(2)]
    pieces = [4, 2]
    firsts = [sum(pieces[:n]) for n in range(len(pieces))]
    l_send = table.add(lambda g, z: [(1 - core(g)) * units])
    l_keep = table.add(lambda g, z: [core(g) * units])

    l_both = [
        table.add(
            lambda g, z, f=f, n=n: [1] * (2 * n)
            + [h * units + f + u for h in (core(g), 1 - core(g)) for u in range(n)]
            + [source for source in (0, 1) for _ in range(n)]
            + [u for _ in (0, 1) for u in range(n)]
        )
        for f, n in zip(firsts, pieces)
    ]
    tab = table.mine()
    order = Order()

    def run(kernel, at, *args):
        return order.done(kernel(order.after(tab), at, *args))

    def add(a, b):
        return order.done(order.after(a) + b)

    def wait(x):
        return order.done(order.after(x))

    embed = (global_embed, embed_local, projection_t)
    state = {"embed": None, "layer": None}
    sizes = [n * UNIT for n in pieces]
    l_got, l_total, l_other = ([None] * len(pieces) for _ in range(3))
    sent, kept, summed, whole_block = ([None] * 2 for _ in range(4))
    came = [[None] * 3, [None] * 3]
    other = [[None] * 3, [None] * 3]

    def layer_send(n):
        l_got[n] = swap_groups(order.after(chip[n]), 2)

    def layer_sum(n):
        l_total[n] = add(chip[n], l_got[n])
        l_other[n] = swap_groups(l_total[n], 1)

    def layer_finish(n):
        sources = (l_total[n], l_other[n])
        state["layer"] = run(
            layer_update, l_both[n], 2 * pieces[n], sources, weights, momentum, groups, state["layer"]
        )

    def project_send(c):
        sent[c] = swap_groups(run(project, p_send[c], 4, tiles[c], *embed), 1)

    def project_keep(c):
        chip = run(project, p_keep[c], 4, tiles[c], *embed, sent[c])
        chip = chip.reshape((4, -1) + chip.shape[1:])
        if c == 1:
            kept[c] = lax.psum_scatter(chip, "tensor", scatter_dimension=0)
        else:
            kept[c] = lax.all_to_all(chip, "tensor", 0, 0)

    def far_send(c):
        kept[c] = wait(kept[c])
        if c == 0:
            kept[c] = order.done((kept[c][0] + kept[c][1]) + (kept[c][2] + kept[c][3]))
        kept[c] = kept[c].reshape(-1, kept[c].shape[-1])
        summed[c] = swap_groups(kept[c], 2)

    def far_sum(c):
        summed[c] = add(kept[c], summed[c])
        other_half = swap_groups(summed[c], 1)
        whole_block[c] = order.done(jnp.concatenate([order.after(summed[c]), other_half]))
        came[c][0] = shift(whole_block[c], 0)

    def step(c, n):
        came[c][n] = wait(came[c][n])
        if n < 2:
            came[c][n + 1] = shift(came[c][n], n + 1)
        other[c][n] = swap_groups(came[c][n], 1)

    def finish(c, at, *sources):
        state["embed"] = run(
            embed_update, at, tiles[c], 4, sources, projection_t, global_embed, embed_momentum, groups,
            state["embed"],
        )

    l_away = swap_groups(run(widen, l_send, [sum(sizes)], local)[0], 1)
    project_send(0)
    chip = run(widen, l_keep, sizes, local, l_away)
    layer_send(0)
    project_keep(0)
    project_send(1)
    project_keep(1)
    layer_sum(0)
    layer_finish(0)
    far_send(0)
    far_sum(0)
    far_send(1)
    step(0, 0)
    far_sum(1)
    finish(0, near[0], whole_block[0], came[0][0], other[0][0])
    step(0, 1)
    step(1, 0)
    layer_send(1)
    finish(1, near[1], whole_block[1], came[1][0], other[1][0])
    step(0, 2)
    step(1, 1)
    finish(0, far[0], came[0][0], other[0][0], came[0][1], other[0][1], came[0][2], other[0][2])
    layer_sum(1)
    step(1, 2)
    finish(1, far[1], came[1][0], other[1][0], came[1][1], other[1][1], came[1][2], other[1][2])
    layer_finish(1)
    new_layer, new_layer_momentum = (x.reshape(global_layer.shape) for x in state["layer"])
    return (new_layer, new_layer_momentum, *state["embed"])


def solution(mesh):
    in_specs = (
        P(None, "tensor", "shards"),
        P("groups", None, "tensor", "shards"),
        P(None, "tensor", "shards"),
        P("shards", "tensor"),
        P("groups", "shards", "tensor"),
        P("shards", "tensor"),
        P("tensor", None),
    )
    out_specs = (
        P(None, "tensor", "shards"),
        P(None, "tensor", "shards"),
        P("shards", "tensor"),
        P("shards", "tensor"),
    )
    return jax.shard_map(body, mesh=mesh, in_specs=in_specs, out_specs=out_specs, check_vma=False)
```

time: 251 us -> 160 us (0.64)
  waiting for transfers between devices: 165 us -> 34.1 us
  Pallas kernels: 0 us -> 72.3 us
  matrix products: 54 us -> 0 us
  starting transfers between devices: 0.26 us -> 26 us
  other arithmetic: 15.7 us -> 4.11 us
  local copies, waits for them, and re-layouts: 2.15 us -> 8.14 us
    psum x2 -> x0, waiting for transfers between devices: 164 us -> none  [the longest x1 107 us: body(): projected = lax.psum(partial_proj, ('groups', 'tensor'))]
    pallas_call x0 -> x12, Pallas kernels: none -> 72.3 us  [the longest x6 43.4 us: update(): pl.pallas_call(functools.partial(update_kernel, at, unit, sub, subs, dept...]
    dot_general x2 -> x0, matrix products: 54 us -> none  [the longest x1 31.9 us: body(): jnp.dot(projected, projection.T, precision=lax.Precision.HIGHEST, preferr...]
    ppermute x0 -> x23, waiting for transfers between devices: none -> 30.5 us  [the longest x17 25.8 us: swap_groups(): return lax.ppermute(x, 'groups', [(g, g ^ bit) for g in range(4)])]
    ppermute x0 -> x23, starting transfers between devices: none -> 21.1 us  [the longest x6 11.8 us: shift(): return lax.ppermute(x, ('groups', 'tensor'), pairs)]
    sub x2 -> x0, other arithmetic: 15.7 us -> none  [the longest x1 10.5 us: nesterov(): return (weights - outer_rate * (delta + momentum_rate * moved), moved)]
    unnamed x6 -> x42, local copies, waits for them, and re-layouts: 2.15 us -> 7.38 us
    all_to_all x0 -> x1, starting transfers between devices: none -> 4.88 us  [project_keep(): kept[c] = lax.all_to_all(chip, 'tensor', 0, 0)]
  transfers between devices with their start and end apart: 2 -> 25, of which waited for: 2 -> 12; matrix products, arithmetic and copies ran while one was open for 15% -> 2% of each run, Pallas kernels for 0% -> 41%
where the time goes in v1:
time: 160 us; the launch traced here: 159 us
  Pallas kernels  72.3 us (45%)
  waiting for transfers between devices  34.1 us (21%)
  starting transfers between devices  26 us (16%)
  between operations  14.5 us (9%)
  local copies, waits for them, and re-layouts  8.14 us (5%)
  other arithmetic  4.11 us (3%)
    pallas_call x6, Pallas kernels, update(): pl.pallas_call(functools.partial(update_kernel, at, unit, sub, subs, dept...  43.4 us
    ppermute x17, waiting for transfers between devices, swap_groups(): return lax.ppermute(x, 'groups', [(g, g ^ bit) for g in range(4)])  25.8 us
    pallas_call x4, Pallas kernels, project(): pl.pallas_call(functools.partial(project_kernel, at, count, tile), in_spe...  21.8 us
    ppermute x6, starting transfers between devices, shift(): return lax.ppermute(x, ('groups', 'tensor'), pairs)  11.8 us
    ppermute x17, starting transfers between devices, swap_groups(): return lax.ppermute(x, 'groups', [(g, g ^ bit) for g in range(4)])  9.28 us
    unnamed x42, local copies, waits for them, and re-layouts  7.38 us
    pallas_call x2, Pallas kernels, widen(): pl.pallas_call(functools.partial(widen_kernel, at, sizes, len(got)), in_s...  7.02 us
    all_to_all x1, starting transfers between devices, project_keep(): kept[c] = lax.all_to_all(chip, 'tensor', 0, 0)  4.88 us
  transfers between devices with their start and end apart: 25, of which 12 were waited for; matrix products, arithmetic and copies ran while one was open for 2% of the time, Pallas kernels for 41%

profile of v1, /device:TPU:0, one launch (start us, length us, event | category | flops | bytes accessed | tf_op | source)
XLA Modules:
  0.0 159.0 jit_solution(14209488663926754831)
XLA Ops:
  7.9 3.3 %widen.2 = f32[1056,512]{1,0:T(8,128)} custom-call(s32[130]{0:T(256)S(1)} %bitcast.22, bf16[2112,512]{1,0:T(8,128)(2,1)} %bitcast.42), custom_call_target="tpu_custom_call" | custom-call | tf_op jit(solution)/shard_map/widen/pallas_call | solution.py:276
  11.7 5.1 %project.4 = f32[2240,128]{1,0:T(8,128)} custom-call(s32[130]{0:T(256)S(1)} %bitcast.23, f32[16000,256]{1,0:T(8,128)} %refs_7_.3, bf16[16000,256]{1,0:T(8,128)(2,1)} %bitcast.34, f32[64,256]{1,0:T(8,128)S(1)} %bitcast.14), custom_call_target="tpu_custom_call" | custom-call | tf_op jit(solution)/shard_map/project/pallas_call | solution.py:104
  18.3 3.7 %widen.3 = (f32[704,512]{1,0:T(8,128)}, f32[352,512]{1,0:T(8,128)S(1)}) custom-call(s32[130]{0:T(256)S(1)} %bitcast.24, bf16[2112,512]{1,0:T(8,128)(2,1)} %bitcast.43, f32[1056,512]{1,0:T(8,128)} %copy-done.7), custom_call_target="tpu_custom_call" | custom-call | tf_op jit(solution)/shard_map/widen/pallas_call | solution.py:276
  22.1 3.0 %collective-permute-start.3 = (f32[704,512]{1,0:T(8,128)}, f32[704,512]{1,0:T(8,128)}, u32[]{:S(2)}, u32[]{:S(2)}) collective-permute-start(f32[704,512]{1,0:T(8,128)} %get-tuple-element.52), channel_id=1, source_target_pairs={{0,16},{8,24},{16,0},{24,8},{1,17},{9,25},{17,1},{25,9},{2,18},{10... | collective-permute-start | bytes 4325384 | tf_op jit(solution)/shard_map/ppermute | solution.py:304
  26.1 6.9 %project.5 = f32[2240,128]{1,0:T(8,128)} custom-call(s32[130]{0:T(256)S(1)} %bitcast.25, f32[16000,256]{1,0:T(8,128)} %refs_7_.3, bf16[16000,256]{1,0:T(8,128)(2,1)} %bitcast.35, f32[64,256]{1,0:T(8,128)S(1)} %bitcast.15, f32[2240,128]{1,0:T(8,128)} %copy-done.9), custom_call_target="tpu_custom_call" | custom-call | tf_op jit(solution)/shard_map/project/pallas_call | solution.py:104
  33.0 3.7 %project.6 = f32[1760,128]{1,0:T(8,128)S(1)} custom-call(s32[130]{0:T(256)S(1)} %bitcast.26, f32[16000,256]{1,0:T(8,128)} %refs_7_.3, bf16[16000,256]{1,0:T(8,128)(2,1)} %bitcast.36, f32[64,256]{1,0:T(8,128)S(1)} %bitcast.16), custom_call_target="tpu_custom_call" | custom-call | tf_op jit(solution)/shard_map/project/pallas_call | solution.py:104
  36.8 4.9 %all-to-all-start = ((f32[4,560,128]{2,1,0:T(8,128)}), f32[4,560,128]{2,1,0:T(8,128)}, u32[]{:S(2)}, u32[]{:S(2)}) async-start(f32[4,560,128]{2,1,0:T(8,128)} %bitcast.7), calls=%async_computation | async-start | bytes 2293760 | tf_op jit(solution)/shard_map/all_to_all | solution.py:440
  42.6 6.1 %project.7 = f32[1760,128]{1,0:T(8,128)} custom-call(s32[130]{0:T(256)S(1)} %bitcast.27, f32[16000,256]{1,0:T(8,128)} %refs_7_.3, bf16[16000,256]{1,0:T(8,128)(2,1)} %bitcast.37, f32[64,256]{1,0:T(8,128)S(1)} %bitcast.17, f32[1760,128]{1,0:T(8,128)} %copy-done.10), custom_call_target="tpu_custom_call" | custom-call | tf_op jit(solution)/shard_map/project/pallas_call | solution.py:104
  48.7 8.5 %collective-permute-done.3 = f32[704,512]{1,0:T(8,128)} collective-permute-done((f32[704,512]{1,0:T(8,128)}, f32[704,512]{1,0:T(8,128)}, u32[]{:S(2)}, u32[]{:S(2)}) %collective-permute-start.3) | collective-permute-done | bytes 1441824 | tf_op jit(solution)/shard_map/ppermute | solution.py:304
  57.2 1.7 %add.36.refs_0_ = f32[704,512]{1,0:T(8,128)S(1)} add(f32[704,512]{1,0:T(8,128)S(1)} %copy-done.8, f32[704,512]{1,0:T(8,128)} %collective-permute-done.3) | non-fusion elementwise | flops 360448 | bytes 4325376 | tf_op jit(solution)/shard_map/add | solution.py:405
  59.0 3.3 %collective-permute-done.4.refs_1_ = f32[704,512]{1,0:T(8,128)} collective-permute-done((f32[704,512]{1,0:T(8,128)S(1)}, f32[704,512]{1,0:T(8,128)}, u32[]{:S(2)}, u32[]{:S(2)}) %collective-permute-start.4) | collective-permute-done | bytes 1441824 | tf_op jit(solution)/shard_map/ppermute | solution.py:304
  62.3 6.8 %layer_update.2 = (f32[2112,512]{1,0:T(8,128)}, f32[2112,512]{1,0:T(8,128)}) custom-call(s32[130]{0:T(256)S(1)} %bitcast.28, f32[704,512]{1,0:T(8,128)} %copy-done.5, f32[704,512]{1,0:T(8,128)} %collective-permute-done.4.refs_1_, f32[2112,512]{1,0:T(8,128)} %bitcast.38, f32[2112,512]{1,0:T(8,128)} %bitcast.40), custom_call_target="tpu_custom_call" | custom-call | tf_op jit(solution)/shard_map/layer_update/pallas_call | solution.py:203
  69.1 2.6 %all-to-all-done = f32[4,560,128]{2,1,0:T(8,128)} async-done(((f32[4,560,128]{2,1,0:T(8,128)}), f32[4,560,128]{2,1,0:T(8,128)}, u32[]{:S(2)}, u32[]{:S(2)}) %all-to-all-start) | async-done | bytes 1146912 | tf_op jit(solution)/shard_map/all_to_all | solution.py:440
  73.0 6.7 %collective-permute-done.5 = f32[560,128]{1,0:T(8,128)S(1)} collective-permute-done((f32[560,128]{1,0:T(8,128)S(1)}, f32[560,128]{1,0:T(8,128)S(1)}, u32[]{:S(2)}, u32[]{:S(2)}) %collective-permute-start.5) | collective-permute-done | bytes 286752 | tf_op jit(solution)/shard_map/ppermute | solution.py:304
  81.4 3.3 %collective-permute-start.7 = (f32[1120,128]{1,0:T(8,128)S(1)}, f32[1120,128]{1,0:T(8,128)S(1)}, u32[]{:S(2)}, u32[]{:S(2)}) collective-permute-start(f32[1120,128]{1,0:T(8,128)S(1)} %constant_dynamic-update-slice_fusion.refs_0_), channel_id=1, source_target_pairs={{0,1},{1,2},{2,3},{9,8},{10,9},{11,10},{16,17},{17,18},{18,19},{25... | collective-permute-start | bytes 1720328 | tf_op jit(solution)/shard_map/ppermute | solution.py:315
  87.3 4.6 %collective-permute-done.7.refs_1_.refs_0_ = f32[1120,128]{1,0:T(8,128)S(1)} collective-permute-done((f32[1120,128]{1,0:T(8,128)S(1)}, f32[1120,128]{1,0:T(8,128)S(1)}, u32[]{:S(2)}, u32[]{:S(2)}) %collective-permute-start.7) | collective-permute-done | bytes 573472 | tf_op jit(solution)/shard_map/ppermute | solution.py:315
  95.9 5.7 %collective-permute-start.10 = (f32[880,128]{1,0:T(8,128)S(1)}, f32[880,128]{1,0:T(8,128)S(1)}, u32[]{:S(2)}, u32[]{:S(2)}) collective-permute-start(f32[880,128]{1,0:T(8,128)S(1)} %constant_dynamic-update-slice_fusion.2.refs_0_), channel_id=1, source_target_pairs={{0,1},{1,2},{2,3},{9,8},{10,9},{11,10},{16,17},{17,18},{18,19},{25... | collective-permute-start | bytes 1351688 | tf_op jit(solution)/shard_map/ppermute | solution.py:315
  102.6 8.9 %embed_update.4 = (f32[16000,256]{1,0:T(8,128)}, f32[16000,256]{1,0:T(8,128)}) custom-call(s32[130]{0:T(256)S(1)} %bitcast.29, f32[1120,128]{1,0:T(8,128)S(1)} %constant_dynamic-update-slice_fusion.refs_0_, f32[1120,128]{1,0:T(8,128)} %copy-done.1, f32[1120,128]{1,0:T(8,128)} %copy-done.6, f32[64,256]{1,0:T(8,128)S(1)} %bitcast.18, f32[16000,256]{1,0:T(8,128)} %refs_7_.3, ...), custom_call_target="tpu_custom_call" | custom-call | tf_op jit(solution)/shard_map/embed_update/pallas_call | solution.py:203
  112.3 1.6 collective-permute-start.19
  116.2 7.6 %embed_update.5 = (f32[16000,256]{1,0:T(8,128)}, f32[16000,256]{1,0:T(8,128)}) custom-call(s32[130]{0:T(256)S(1)} %bitcast.30, f32[880,128]{1,0:T(8,128)S(1)} %constant_dynamic-update-slice_fusion.2.refs_0_, f32[880,128]{1,0:T(8,128)S(1)} %collective-permute-done.10.refs_1_.refs_0_, ...), custom_call_target="tpu_custom_call", output_to_operand_aliasing={{0}: (7, {}), {1}: (8, {})} | custom-call | tf_op jit(solution)/shard_map/embed_update/pallas_call | solution.py:203
  126.7 8.7 %embed_update.6 = (f32[16000,256]{1,0:T(8,128)}, f32[16000,256]{1,0:T(8,128)}) custom-call(s32[130]{0:T(256)S(1)} %bitcast.31, f32[1120,128]{1,0:T(8,128)S(1)} %copy-done.2, f32[1120,128]{1,0:T(8,128)} %copy-done.6, f32[1120,128]{1,0:T(8,128)} %copy-done.12, f32[1120,128]{1,0:T(8,128)} %copy-done.14, ...), custom_call_target="tpu_custom_call", output_to_operand_aliasing={{0}: (10, {}), {1}: (11, {})} | custom-call | tf_op jit(solution)/shard_map/embed_update/pallas_call | solution.py:203
  136.3 2.2 %collective-permute-done.20.refs_3_ = f32[880,128]{1,0:T(8,128)S(1)} collective-permute-done((f32[880,128]{1,0:T(8,128)S(1)}, f32[880,128]{1,0:T(8,128)S(1)}, u32[]{:S(2)}, u32[]{:S(2)}) %collective-permute-start.20) | collective-permute-done | bytes 450592 | tf_op jit(solution)/shard_map/ppermute | solution.py:304
  139.9 7.5 %embed_update.7 = (f32[16000,256]{1,0:T(8,128)}, f32[16000,256]{1,0:T(8,128)}) custom-call(s32[130]{0:T(256)S(1)} %bitcast.32, f32[880,128]{1,0:T(8,128)S(1)} %collective-permute-done.10.refs_1_.refs_0_, f32[880,128]{1,0:T(8,128)S(1)} %copy-done.4, f32[880,128]{1,0:T(8,128)} %copy-done.16, ...), custom_call_target="tpu_custom_call", output_to_operand_aliasing={{0}: (10, {}), {1}: (11, {})} | custom-call | tf_op jit(solution)/shard_map/embed_update/pallas_call | solution.py:203
  148.3 3.9 %layer_update.3 = (f32[2112,512]{1,0:T(8,128)}, f32[2112,512]{1,0:T(8,128)}) custom-call(s32[130]{0:T(256)S(1)} %bitcast.33, f32[352,512]{1,0:T(8,128)S(1)} %add.43.refs_0_, f32[352,512]{1,0:T(8,128)} %copy-done.11, f32[2112,512]{1,0:T(8,128)} %bitcast.39, f32[2112,512]{1,0:T(8,128)} %bitcast.41, ...), custom_call_target="tpu_custom_call", output_to_operand_aliasing={{0}: (5, {}), {1}: (6, {})} | custom-call | tf_op jit(solution)/shard_map/layer_update/pallas_call | solution.py:203
  (89 shorter events, 24.2 us)
Async XLA Ops:
  11.2 5.8 %collective-permute-start = (f32[1056,512]{1,0:T(8,128)}, f32[1056,512]{1,0:T(8,128)S(1)}, u32[]{:S(2)}, u32[]{:S(2)}) collective-permute-start(f32[1056,512]{1,0:T(8,128)} %widen.2), channel_id=1, source_target_pairs={{0,8},{8,0},{16,24},{24,16},{1,9},{9,1},{17,25},{25,17},{2,10},{10... | collective-permute-start | bytes 6488072 | tf_op jit(solution)/shard_map/ppermute | solution.py:304
  16.9 8.2 %collective-permute-start.1 = (f32[2240,128]{1,0:T(8,128)}, f32[2240,128]{1,0:T(8,128)S(1)}, u32[]{:S(2)}, u32[]{:S(2)}) collective-permute-start(f32[2240,128]{1,0:T(8,128)} %project.4), channel_id=1, source_target_pairs={{0,8},{8,0},{16,24},{24,16},{1,9},{9,1},{17,25},{25,17},{2,10},{10... | collective-permute-start | bytes 3440648 | tf_op jit(solution)/shard_map/ppermute | solution.py:304
  22.1 35.1 %collective-permute-start.3 = (f32[704,512]{1,0:T(8,128)}, f32[704,512]{1,0:T(8,128)}, u32[]{:S(2)}, u32[]{:S(2)}) collective-permute-start(f32[704,512]{1,0:T(8,128)} %get-tuple-element.52), channel_id=1, source_target_pairs={{0,16},{8,24},{16,0},{24,8},{1,17},{9,25},{17,1},{25,9},{2,18},{10... | collective-permute-start | bytes 4325384 | tf_op jit(solution)/shard_map/ppermute | solution.py:304
  36.7 5.0 %collective-permute-start.2 = (f32[1760,128]{1,0:T(8,128)S(1)}, f32[1760,128]{1,0:T(8,128)S(1)}, u32[]{:S(2)}, u32[]{:S(2)}) collective-permute-start(f32[1760,128]{1,0:T(8,128)S(1)} %project.6), channel_id=1, source_target_pairs={{0,8},{8,0},{16,24},{24,16},{1,9},{9,1},{17,25},{25,17},{2,10},{10... | collective-permute-start | bytes 2703368 | tf_op jit(solution)/shard_map/ppermute | solution.py:304
  36.8 34.9 %all-to-all-start = ((f32[4,560,128]{2,1,0:T(8,128)}), f32[4,560,128]{2,1,0:T(8,128)}, u32[]{:S(2)}, u32[]{:S(2)}) async-start(f32[4,560,128]{2,1,0:T(8,128)} %bitcast.7), calls=%async_computation | async-start | bytes 2293760 | tf_op jit(solution)/shard_map/all_to_all | solution.py:440
  41.7 44.1 %reduce-scatter.4.cloned.1.call-start = ((), (), s32[]{:S(2)}) async-start(), calls=%async_computation.2 | async-start | bytes 1126400
  58.9 3.4 %collective-permute-start.4 = (f32[704,512]{1,0:T(8,128)S(1)}, f32[704,512]{1,0:T(8,128)}, u32[]{:S(2)}, u32[]{:S(2)}) collective-permute-start(f32[704,512]{1,0:T(8,128)S(1)} %add.36.refs_0_), channel_id=1, source_target_pairs={{0,8},{8,0},{16,24},{24,16},{1,9},{9,1},{17,25},{25,17},{2,10},{10... | collective-permute-start | bytes 4325384 | tf_op jit(solution)/shard_map/ppermute | solution.py:304
  73.0 6.8 %collective-permute-start.5 = (f32[560,128]{1,0:T(8,128)S(1)}, f32[560,128]{1,0:T(8,128)S(1)}, u32[]{:S(2)}, u32[]{:S(2)}) collective-permute-start(f32[560,128]{1,0:T(8,128)S(1)} %add_bitcast_fusion), channel_id=1, source_target_pairs={{0,16},{8,24},{16,0},{24,8},{1,17},{9,25},{17,1},{25,9},{2,18},{10... | collective-permute-start | bytes 860168 | tf_op jit(solution)/shard_map/ppermute | solution.py:304
  79.8 1.6 %collective-permute-start.6 = (f32[560,128]{1,0:T(8,128)S(1)}, f32[560,128]{1,0:T(8,128)S(1)}, u32[]{:S(2)}, u32[]{:S(2)}) collective-permute-start(f32[560,128]{1,0:T(8,128)S(1)} %add.41), channel_id=1, source_target_pairs={{0,8},{8,0},{16,24},{24,16},{1,9},{9,1},{17,25},{25,17},{2,10},{10... | collective-permute-start | bytes 860168 | tf_op jit(solution)/shard_map/ppermute | solution.py:304
  81.4 10.5 %collective-permute-start.7 = (f32[1120,128]{1,0:T(8,128)S(1)}, f32[1120,128]{1,0:T(8,128)S(1)}, u32[]{:S(2)}, u32[]{:S(2)}) collective-permute-start(f32[1120,128]{1,0:T(8,128)S(1)} %constant_dynamic-update-slice_fusion.refs_0_), channel_id=1, source_target_pairs={{0,1},{1,2},{2,3},{9,8},{10,9},{11,10},{16,17},{17,18},{18,19},{25... | collective-permute-start | bytes 1720328 | tf_op jit(solution)/shard_map/ppermute | solution.py:315
  85.8 7.6 %collective-permute-start.8 = (f32[440,128]{1,0:T(8,128)}, f32[440,128]{1,0:T(8,128)S(1)}, u32[]{:S(2)}, u32[]{:S(2)}) collective-permute-start(f32[440,128]{1,0:T(8,128)} %bitcast.46), channel_id=1, source_target_pairs={{0,16},{8,24},{16,0},{24,8},{1,17},{9,25},{17,1},{25,9},{2,18},{10... | collective-permute-start | bytes 675848 | tf_op jit(solution)/shard_map/ppermute | solution.py:304
  94.5 7.2 %collective-permute-start.12 = (f32[1120,128]{1,0:T(8,128)S(1)}, f32[1120,128]{1,0:T(8,128)S(1)}, u32[]{:S(2)}, u32[]{:S(2)}) collective-permute-start(f32[1120,128]{1,0:T(8,128)S(1)} %collective-permute-done.7.refs_1_.refs_0_), channel_id=1, source_target_pairs={{0,8},{8,0},{16,24},{24,16},{1,9},{9,1},{17,25},{25,17},{2,10},{10... | collective-permute-start | bytes 1720328 | tf_op jit(solution)/shard_map/ppermute | solution.py:304
  95.0 16.5 %collective-permute-start.11 = (f32[1120,128]{1,0:T(8,128)S(1)}, f32[1120,128]{1,0:T(8,128)S(1)}, u32[]{:S(2)}, u32[]{:S(2)}) collective-permute-start(f32[1120,128]{1,0:T(8,128)S(1)} %collective-permute-done.7.refs_1_.refs_0_), channel_id=1, source_target_pairs={{1,2},{2,3},{9,8},{10,9},{17,18},{18,19},{25,24},{26,25},{5,6},{6,... | collective-permute-start | bytes 1720328 | tf_op jit(solution)/shard_map/ppermute | solution.py:315
  95.9 16.3 %collective-permute-start.10 = (f32[880,128]{1,0:T(8,128)S(1)}, f32[880,128]{1,0:T(8,128)S(1)}, u32[]{:S(2)}, u32[]{:S(2)}) collective-permute-start(f32[880,128]{1,0:T(8,128)S(1)} %constant_dynamic-update-slice_fusion.2.refs_0_), channel_id=1, source_target_pairs={{0,1},{1,2},{2,3},{9,8},{10,9},{11,10},{16,17},{17,18},{18,19},{25... | collective-permute-start | bytes 1351688 | tf_op jit(solution)/shard_map/ppermute | solution.py:315
  111.5 12.3 %collective-permute-start.14 = (f32[1120,128]{1,0:T(8,128)S(1)}, f32[1120,128]{1,0:T(8,128)S(1)}, u32[]{:S(2)}, u32[]{:S(2)}) collective-permute-start(f32[1120,128]{1,0:T(8,128)S(1)} %collective-permute-done.11.refs_2_), channel_id=1, source_target_pairs={{2,3},{9,8},{18,19},{25,24},{6,7},{13,12},{22,23},{29,28}} | collective-permute-start | bytes 1720328 | tf_op jit(solution)/shard_map/ppermute | solution.py:315
  112.2 3.2 %collective-permute-start.15 = (f32[880,128]{1,0:T(8,128)S(1)}, f32[880,128]{1,0:T(8,128)S(1)}, u32[]{:S(2)}, u32[]{:S(2)}) collective-permute-start(f32[880,128]{1,0:T(8,128)S(1)} %collective-permute-done.10.refs_1_.refs_0_), channel_id=1, source_target_pairs={{0,8},{8,0},{16,24},{24,16},{1,9},{9,1},{17,25},{25,17},{2,10},{10... | collective-permute-start | bytes 1351688 | tf_op jit(solution)/shard_map/ppermute | solution.py:304
  112.3 23.1 %collective-permute-start.19 = (f32[352,512]{1,0:T(8,128)S(1)}, f32[352,512]{1,0:T(8,128)S(1)}, u32[]{:S(2)}, u32[]{:S(2)}) collective-permute-start(f32[352,512]{1,0:T(8,128)S(1)} %get-tuple-element.76), channel_id=1, source_target_pairs={{0,16},{8,24},{16,0},{24,8},{1,17},{9,25},{17,1},{25,9},{2,18},{10... | collective-permute-start | bytes 2162696 | tf_op jit(solution)/shard_map/ppermute | solution.py:304
  113.9 10.0 %collective-permute-start.13 = (f32[880,128]{1,0:T(8,128)S(1)}, f32[880,128]{1,0:T(8,128)S(1)}, u32[]{:S(2)}, u32[]{:S(2)}) collective-permute-start(f32[880,128]{1,0:T(8,128)S(1)} %collective-permute-done.10.refs_1_.refs_0_), channel_id=1, source_target_pairs={{1,2},{2,3},{9,8},{10,9},{17,18},{18,19},{25,24},{26,25},{5,6},{6,... | collective-permute-start | bytes 1351688 | tf_op jit(solution)/shard_map/ppermute | solution.py:315
  114.6 10.0 %collective-permute-start.17 = (f32[1120,128]{1,0:T(8,128)S(1)}, f32[1120,128]{1,0:T(8,128)S(1)}, u32[]{:S(2)}, u32[]{:S(2)}) collective-permute-start(f32[1120,128]{1,0:T(8,128)S(1)} %collective-permute-done.11.refs_2_), channel_id=1, source_target_pairs={{0,8},{8,0},{16,24},{24,16},{1,9},{9,1},{17,25},{25,17},{2,10},{10... | collective-permute-start | bytes 1720328 | tf_op jit(solution)/shard_map/ppermute | solution.py:304
  123.8 2.0 %collective-permute-start.18 = (f32[1120,128]{1,0:T(8,128)S(1)}, f32[1120,128]{1,0:T(8,128)S(1)}, u32[]{:S(2)}, u32[]{:S(2)}) collective-permute-start(f32[1120,128]{1,0:T(8,128)S(1)} %collective-permute-done.14.refs_4_), channel_id=1, source_target_pairs={{0,8},{8,0},{16,24},{24,16},{1,9},{9,1},{17,25},{25,17},{2,10},{10... | collective-permute-start | bytes 1720328 | tf_op jit(solution)/shard_map/ppermute | solution.py:304
  123.9 12.2 %collective-permute-start.16 = (f32[880,128]{1,0:T(8,128)S(1)}, f32[880,128]{1,0:T(8,128)S(1)}, u32[]{:S(2)}, u32[]{:S(2)}) collective-permute-start(f32[880,128]{1,0:T(8,128)S(1)} %collective-permute-done.13.refs_2_), channel_id=1, source_target_pairs={{2,3},{9,8},{18,19},{25,24},{6,7},{13,12},{22,23},{29,28}} | collective-permute-start | bytes 1351688 | tf_op jit(solution)/shard_map/ppermute | solution.py:315
  135.5 11.9 %collective-permute-start.22 = (f32[352,512]{1,0:T(8,128)S(1)}, f32[352,512]{1,0:T(8,128)S(1)}, u32[]{:S(2)}, u32[]{:S(2)}) collective-permute-start(f32[352,512]{1,0:T(8,128)S(1)} %add.43.refs_0_), channel_id=1, source_target_pairs={{0,8},{8,0},{16,24},{24,16},{1,9},{9,1},{17,25},{25,17},{2,10},{10... | collective-permute-start | bytes 2162696 | tf_op jit(solution)/shard_map/ppermute | solution.py:304
  135.7 2.7 %collective-permute-start.20 = (f32[880,128]{1,0:T(8,128)S(1)}, f32[880,128]{1,0:T(8,128)S(1)}, u32[]{:S(2)}, u32[]{:S(2)}) collective-permute-start(f32[880,128]{1,0:T(8,128)S(1)} %collective-permute-done.13.refs_2_), channel_id=1, source_target_pairs={{0,8},{8,0},{16,24},{24,16},{1,9},{9,1},{17,25},{25,17},{2,10},{10... | collective-permute-start | bytes 1351688 | tf_op jit(solution)/shard_map/ppermute | solution.py:304
  136.1 3.0 %collective-permute-start.21 = (f32[880,128]{1,0:T(8,128)S(1)}, f32[880,128]{1,0:T(8,128)S(1)}, u32[]{:S(2)}, u32[]{:S(2)}) collective-permute-start(f32[880,128]{1,0:T(8,128)S(1)} %collective-permute-done.16.refs_4_), channel_id=1, source_target_pairs={{0,8},{8,0},{16,24},{24,16},{1,9},{9,1},{17,25},{25,17},{2,10},{10... | collective-permute-start | bytes 1351688 | tf_op jit(solution)/shard_map/ppermute | solution.py:304
  (21 other events, 97.0 us)
Sparse Core Ops, SparseCore 0:
  59.1 26.6 reduce-scatter.3

commit v2 on v1

--- a/solution.py
+++ b/solution.py
@@ -76,17 +76,11 @@
         for copy in pair:
             copy.start()
         copies.append(pair)
-    if len(refs) > 7:
-        add = pltpu.make_async_copy(refs[0], out, p_sem)
     fetch.wait()
-    if len(refs) > 7:
-        add.start()
     high, low = (x.T for x in halves(p_in[...]))
     none = jnp.zeros_like(high)
     w[0:width] = jnp.concatenate([high, none, low, none], axis=1)
     w[width:] = jnp.concatenate([none, high, none, low], axis=1)
-    if len(refs) > 7:
-        add.wait()
     for i in range(count):
         for copy in copies[i]:
             copy.wait()
@@ -95,7 +89,7 @@
         wide = dot(high, w[...])
         mine = wide[:, 0 : 2 * rank] + wide[:, 2 * rank :] + dot(low, w[:, 0 : 2 * rank])
         rows = slice(i * half, (i + 1) * half)
-        out[rows] = mine + out[rows] if len(refs) > 7 else mine
+        out[rows] = mine + refs[0][rows] if len(refs) > 7 else mine
 
 
 def project(tab, at, count, tile, global_embed, local_embed, projection_t, *got):
@@ -103,7 +97,7 @@
     rank = projection_t.shape[0]
     return pl.pallas_call(
         functools.partial(project_kernel, at, count, tile),
-        in_specs=[SMEM, HBM, HBM, HBM] + [ANY] * len(got),
+        in_specs=[SMEM, HBM, HBM, HBM] + [VMEM] * len(got),
         out_specs=VMEM,
         out_shape=jax.ShapeDtypeStruct((count * tile // 2, 2 * rank), jnp.float32),
         scratch_shapes=[
@@ -256,30 +250,27 @@
     )
 
 
-def widen_kernel(at, sizes, added, tab, l, *refs):
-    got, outs, (l_in, sem), near = refs[:added], refs[added : -2 - added], refs[-2 - added :][:2], refs[len(refs) - added :]
-    copies = [pltpu.make_async_copy(rows_at(l, tab[at], UNIT, 0, sum(sizes)), l_in, sem.at[0])]
-    copies += [pltpu.make_async_copy(x, to, sem.at[1]) for x, to in zip(got, near)]
-    for copy in copies:
-        copy.start()
-    for copy in copies:
-        copy.wait()
+def widen_kernel(at, sizes, tab, l, *refs):
+    *got, l_in, sem = refs
+    got, outs = got[: len(got) - len(sizes)], got[len(got) - len(sizes) :]
+    copy = pltpu.make_async_copy(rows_at(l, tab[at], UNIT, 0, sum(sizes)), l_in, sem)
+    copy.start()
+    copy.wait()
     first = 0
     for out, size in zip(outs, sizes):
         value = l_in[first : first + size].astype(jnp.float32)
-        out[...] = value + near[0][first : first + size] if added else value
+        out[...] = value + got[0][first : first + size] if got else value
         first += size
 
 
 def widen(tab, at, sizes, local, *got):
     width = local.shape[1]
     return pl.pallas_call(
-        functools.partial(widen_kernel, at, sizes, len(got)),
-        in_specs=[SMEM, HBM] + [ANY] * len(got),
+        functools.partial(widen_kernel, at, sizes),
+        in_specs=[SMEM, HBM] + [VMEM] * len(got),
         out_specs=[VMEM] * len(sizes),
         out_shape=[jax.ShapeDtypeStruct((size, width), jnp.float32) for size in sizes],
-        scratch_shapes=[pltpu.VMEM((sum(sizes), width), jnp.bfloat16), pltpu.SemaphoreType.DMA((2,))]
-        + [pltpu.VMEM(x.shape, x.dtype) for x in got],
+        scratch_shapes=[pltpu.VMEM((sum(sizes), width), jnp.bfloat16), pltpu.SemaphoreType.DMA(())],
         compiler_params=PARAMS,
         cost_estimate=COST,
         name="widen",
@@ -363,7 +354,7 @@
     p_send = [table.add(lambda g, z, c=c: [place(c, 1 - core(g), k) for k in range(4)]) for c in range(2)]
     p_keep = [table.add(lambda g, z, c=c: [place(c, core(g), k) for k in range(4)]) for c in range(2)]
 
-    def blocks_at(c, first):
+    def blocks_at(c, turn):
         def entry(g, z):
             blocks = []
             for n in range(4):
@@ -371,30 +362,28 @@
                     k = 2 * z - k if core(g) else k
                     if n or h == core(g):
                         blocks.append((len(blocks), h, k))
-            beside = [b for b in blocks[1:3] if 0 <= b[2] < 4][0]
-            early = [blocks[0], beside]
-            turn = early if first else [b for b in blocks if b not in early and 0 <= b[2] < 4]
-            parts = [(place(c, h ^ half, k), n if first else n - 1, half) for n, h, k in turn for half in (0, 1)]
+            there = [b for b in blocks if 0 <= b[2] < 4]
+            taken = (there[:1], there[1:2], there[2:], there[:2])[turn]
+            parts = [(place(c, h ^ half, k), n - (turn in (1, 2)), half) for n, h, k in taken for half in (0, 1)]
             return [1] * len(parts) + [p for column in zip(*parts) for p in column]
 
         return table.add(entry)
 
-    near = [blocks_at(c, True) for c in range(2)]
-    far = [blocks_at(c, False) for c in range(2)]
-    pieces = [4, 2]
+    own, beside, far, near = ([blocks_at(c, turn) for c in range(2)] for turn in range(4))
+    pieces = [3, 3]
     firsts = [sum(pieces[:n]) for n in range(len(pieces))]
     l_send = table.add(lambda g, z: [(1 - core(g)) * units])
     l_keep = table.add(lambda g, z: [core(g) * units])
 
-    l_both = [
-        table.add(
-            lambda g, z, f=f, n=n: [1] * (2 * n)
-            + [h * units + f + u for h in (core(g), 1 - core(g)) for u in range(n)]
-            + [source for source in (0, 1) for _ in range(n)]
-            + [u for _ in (0, 1) for u in range(n)]
-        )
-        for f, n in zip(firsts, pieces)
-    ]
+
+    def l_entry(g, z):
+        parts = []
+        for n, (f, size) in enumerate(zip(firsts, pieces)):
+            for h in (0, 1):
+                parts += [((core(g) ^ h) * units + f + u, 2 * n + h, u) for u in range(size)]
+        return [1] * len(parts) + [p for column in zip(*parts) for p in column]
+
+    l_all = table.add(l_entry)
     tab = table.mine()
     order = Order()
 
@@ -422,11 +411,9 @@
         l_total[n] = add(chip[n], l_got[n])
         l_other[n] = swap_groups(l_total[n], 1)
 
-    def layer_finish(n):
-        sources = (l_total[n], l_other[n])
-        state["layer"] = run(
-            layer_update, l_both[n], 2 * pieces[n], sources, weights, momentum, groups, state["layer"]
-        )
+    def layer_finish():
+        sources = [x for pair in zip(l_total, l_other) for x in pair]
+        state["layer"] = run(layer_update, l_all, 2 * units, sources, weights, momentum, groups, state["layer"])
 
     def project_send(c):
         sent[c] = swap_groups(run(project, p_send[c], 4, tiles[c], *embed), 1)
@@ -434,22 +421,24 @@
     def project_keep(c):
         chip = run(project, p_keep[c], 4, tiles[c], *embed, sent[c])
         chip = chip.reshape((4, -1) + chip.shape[1:])
-        if c == 1:
+        if c == 0:
             kept[c] = lax.psum_scatter(chip, "tensor", scatter_dimension=0)
         else:
             kept[c] = lax.all_to_all(chip, "tensor", 0, 0)
 
     def far_send(c):
         kept[c] = wait(kept[c])
-        if c == 0:
+        if c == 1:
             kept[c] = order.done((kept[c][0] + kept[c][1]) + (kept[c][2] + kept[c][3]))
         kept[c] = kept[c].reshape(-1, kept[c].shape[-1])
         summed[c] = swap_groups(kept[c], 2)
 
     def far_sum(c):
         summed[c] = add(kept[c], summed[c])
-        other_half = swap_groups(summed[c], 1)
-        whole_block[c] = order.done(jnp.concatenate([order.after(summed[c]), other_half]))
+        whole_block[c] = swap_groups(summed[c], 1)
+
+    def spread(c):
+        whole_block[c] = order.done(jnp.concatenate([order.after(summed[c]), whole_block[c]]))
         came[c][0] = shift(whole_block[c], 0)
 
     def step(c, n):
@@ -458,38 +447,43 @@
             came[c][n + 1] = shift(came[c][n], n + 1)
         other[c][n] = swap_groups(came[c][n], 1)
 
-    def finish(c, at, *sources):
+    def finish(c, at, count, *sources):
         state["embed"] = run(
-            embed_update, at, tiles[c], 4, sources, projection_t, global_embed, embed_momentum, groups,
+            embed_update, at[c], tiles[c], count, sources, projection_t, global_embed, embed_momentum, groups,
             state["embed"],
         )
 
+    def received(c, steps):
+        return [x for n in range(steps) for x in (came[c][n], other[c][n])]
+
+    project_send(0)
     l_away = swap_groups(run(widen, l_send, [sum(sizes)], local)[0], 1)
-    project_send(0)
+    project_keep(0)
+    project_send(1)
     chip = run(widen, l_keep, sizes, local, l_away)
     layer_send(0)
-    project_keep(0)
-    project_send(1)
     project_keep(1)
+    far_send(0)
     layer_sum(0)
-    layer_finish(0)
-    far_send(0)
     far_sum(0)
+    spread(0)
     far_send(1)
+    finish(0, own, 2, whole_block[0])
     step(0, 0)
     far_sum(1)
-    finish(0, near[0], whole_block[0], came[0][0], other[0][0])
+    spread(1)
+    finish(0, beside, 2, *received(0, 1))
     step(0, 1)
     step(1, 0)
     layer_send(1)
-    finish(1, near[1], whole_block[1], came[1][0], other[1][0])
+    finish(1, near, 4, whole_block[1], *received(1, 1))
     step(0, 2)
     step(1, 1)
-    finish(0, far[0], came[0][0], other[0][0], came[0][1], other[0][1], came[0][2], other[0][2])
+    finish(0, far, 4, *received(0, 3))
+    step(1, 2)
     layer_sum(1)
-    step(1, 2)
-    finish(1, far[1], came[1][0], other[1][0], came[1][1], other[1][1], came[1][2], other[1][2])
-    layer_finish(1)
+    finish(1, far, 4, *received(1, 3))
+    layer_finish()
     new_layer, new_layer_momentum = (x.reshape(global_layer.shape) for x in state["layer"])
     return (new_layer, new_layer_momentum, *state["embed"])
 

time: 160 us -> 155 us (0.969)
  waiting for transfers between devices: 34.1 us -> 21.8 us
  starting transfers between devices: 26 us -> 33.8 us
    ppermute x17, waiting for transfers between devices: 25.8 us -> 11.6 us  [swap_groups(): return lax.ppermute(x, 'groups', [(g, g ^ bit) for g in range(4)])]
    reduce_scatter x0 -> x1, waiting for transfers between devices: none -> 9.87 us  [project_keep(): kept[c] = lax.psum_scatter(chip, 'tensor', scatter_dimension=0)]
    ppermute x17, starting transfers between devices: 9.28 us -> 15.5 us  [swap_groups(): return lax.ppermute(x, 'groups', [(g, g ^ bit) for g in range(4)])]
    ppermute x6, waiting for transfers between devices: 4.66 us -> 0.35 us  [shift(): return lax.ppermute(x, ('groups', 'tensor'), pairs)]
    all_to_all x1, waiting for transfers between devices: 2.58 us -> 0.01 us  [project_keep(): kept[c] = lax.all_to_all(chip, 'tensor', 0, 0)]
    pallas_call x4, Pallas kernels: 21.8 us -> 19.9 us  [project(): pl.pallas_call(functools.partial(project_kernel, at, count, tile), in_spe...]
    ppermute x6, starting transfers between devices: 11.8 us -> 13.4 us  [shift(): return lax.ppermute(x, ('groups', 'tensor'), pairs)]
    unnamed x42 -> x44, local copies, waits for them, and re-layouts: 7.38 us -> 8.81 us
  transfers between devices with their start and end apart: 25 -> 25, of which waited for: 12 -> 11; matrix products, arithmetic and copies ran while one was open for 2% -> 2% of each run, Pallas kernels for 41% -> 37%
where the time goes in v2:
time: 155 us; the launch traced here: 154 us
  Pallas kernels  71 us (46%)
  starting transfers between devices  33.8 us (22%)
  waiting for transfers between devices  21.8 us (14%)
  between operations  14.5 us (9%)
  local copies, waits for them, and re-layouts  9.55 us (6%)
  other arithmetic  3.05 us (2%)
    pallas_call x6, Pallas kernels, update(): pl.pallas_call(functools.partial(update_kernel, at, unit, sub, subs, dept...  43.5 us
    pallas_call x4, Pallas kernels, project(): pl.pallas_call(functools.partial(project_kernel, at, count, tile), in_spe...  19.9 us
    ppermute x17, starting transfers between devices, swap_groups(): return lax.ppermute(x, 'groups', [(g, g ^ bit) for g in range(4)])  15.5 us
    ppermute x6, starting transfers between devices, shift(): return lax.ppermute(x, ('groups', 'tensor'), pairs)  13.4 us
    ppermute x17, waiting for transfers between devices, swap_groups(): return lax.ppermute(x, 'groups', [(g, g ^ bit) for g in range(4)])  11.6 us
    reduce_scatter x1, waiting for transfers between devices, project_keep(): kept[c] = lax.psum_scatter(chip, 'tensor', scatter_dimension=0)  9.87 us
    unnamed x44, local copies, waits for them, and re-layouts  8.81 us
    pallas_call x2, Pallas kernels, widen(): pl.pallas_call(functools.partial(widen_kernel, at, sizes), in_specs=[SMEM...  7.57 us
  transfers between devices with their start and end apart: 25, of which 11 were waited for; matrix products, arithmetic and copies ran while one was open for 2% of the time, Pallas kernels for 37%

profile of v2, /device:TPU:0, one launch (start us, length us, event | category | flops | bytes accessed | tf_op | source)
XLA Modules:
  0.0 153.7 jit_solution(7313678315273637377)
XLA Ops:
  8.8 5.1 %project.4 = f32[2240,128]{1,0:T(8,128)} custom-call(s32[162]{0:T(256)S(1)} %bitcast.22, f32[16000,256]{1,0:T(8,128)} %refs_7_.3, bf16[16000,256]{1,0:T(8,128)(2,1)} %bitcast.34, f32[64,256]{1,0:T(8,128)S(1)} %bitcast.13), custom_call_target="tpu_custom_call" | custom-call | tf_op jit(solution)/shard_map/project/pallas_call | solution.py:98
  14.4 3.3 %widen.2 = f32[1056,512]{1,0:T(8,128)} custom-call(s32[162]{0:T(256)S(1)} %bitcast.23, bf16[2112,512]{1,0:T(8,128)(2,1)} %bitcast.38), custom_call_target="tpu_custom_call" | custom-call | tf_op jit(solution)/shard_map/widen/pallas_call | solution.py:268
  18.8 5.8 %project.5 = f32[2240,128]{1,0:T(8,128)} custom-call(s32[162]{0:T(256)S(1)} %bitcast.24, f32[16000,256]{1,0:T(8,128)} %refs_7_.3, bf16[16000,256]{1,0:T(8,128)(2,1)} %bitcast.35, f32[64,256]{1,0:T(8,128)S(1)} %bitcast.14, f32[2240,128]{1,0:T(8,128)} %copy-done.8), custom_call_target="tpu_custom_call" | custom-call | tf_op jit(solution)/shard_map/project/pallas_call | solution.py:98
  24.7 3.7 %project.6 = f32[1760,128]{1,0:T(8,128)S(1)} custom-call(s32[162]{0:T(256)S(1)} %bitcast.25, f32[16000,256]{1,0:T(8,128)} %refs_7_.3, bf16[16000,256]{1,0:T(8,128)(2,1)} %bitcast.36, f32[64,256]{1,0:T(8,128)S(1)} %bitcast.15), custom_call_target="tpu_custom_call" | custom-call | tf_op jit(solution)/shard_map/project/pallas_call | solution.py:98
  30.3 4.3 %widen.3 = (f32[528,512]{1,0:T(8,128)}, f32[528,512]{1,0:T(8,128)}) custom-call(s32[162]{0:T(256)S(1)} %bitcast.26, bf16[2112,512]{1,0:T(8,128)(2,1)} %bitcast.39, f32[1056,512]{1,0:T(8,128)} %copy-done.7), custom_call_target="tpu_custom_call" | custom-call | tf_op jit(solution)/shard_map/widen/pallas_call | solution.py:268
  34.6 2.7 %collective-permute-start.3 = (f32[528,512]{1,0:T(8,128)}, f32[528,512]{1,0:T(8,128)}, u32[]{:S(2)}, u32[]{:S(2)}) collective-permute-start(f32[528,512]{1,0:T(8,128)} %get-tuple-element.54), channel_id=1, source_target_pairs={{0,16},{8,24},{16,0},{24,8},{1,17},{9,25},{17,1},{25,9},{2,18},{10... | collective-permute-start | bytes 3244040 | tf_op jit(solution)/shard_map/ppermute | solution.py:295
  38.3 5.3 %project.7 = f32[1760,128]{1,0:T(8,128)} custom-call(s32[162]{0:T(256)S(1)} %bitcast.27, f32[16000,256]{1,0:T(8,128)} %refs_7_.3, bf16[16000,256]{1,0:T(8,128)(2,1)} %bitcast.37, f32[64,256]{1,0:T(8,128)S(1)} %bitcast.16, f32[1760,128]{1,0:T(8,128)} %copy-done.12), custom_call_target="tpu_custom_call" | custom-call | tf_op jit(solution)/shard_map/project/pallas_call | solution.py:98
  43.5 4.9 %all-to-all-start = ((f32[4,440,128]{2,1,0:T(8,128)}), f32[4,440,128]{2,1,0:T(8,128)S(1)}, u32[]{:S(2)}, u32[]{:S(2)}) async-start(f32[4,440,128]{2,1,0:T(8,128)} %bitcast.4), calls=%async_computation | async-start | bytes 1802240 | tf_op jit(solution)/shard_map/all_to_all | solution.py:427
  48.4 9.9 %reduce-scatter.2.cloned.1.call-done = f32[1,560,128]{2,1,0:T(8,128)} async-done(((f32[4,560,128]{2,1,0:T(8,128)}), f32[1,560,128]{2,1,0:T(8,128)}) %reduce-scatter.2.cloned.1.call-update) | async-done | bytes 286736 | tf_op jit(solution)/shard_map/reduce_scatter | solution.py:425
  58.3 2.4 %collective-permute-start.4 = (f32[560,128]{1,0:T(8,128)}, f32[560,128]{1,0:T(8,128)S(1)}, u32[]{:S(2)}, u32[]{:S(2)}) collective-permute-start(f32[560,128]{1,0:T(8,128)} %bitcast.43), channel_id=1, source_target_pairs={{0,16},{8,24},{16,0},{24,8},{1,17},{9,25},{17,1},{25,9},{2,18},{10... | collective-permute-start | bytes 860168 | tf_op jit(solution)/shard_map/ppermute | solution.py:295
  60.7 1.7 %collective-permute-done.3 = f32[528,512]{1,0:T(8,128)} collective-permute-done((f32[528,512]{1,0:T(8,128)}, f32[528,512]{1,0:T(8,128)}, u32[]{:S(2)}, u32[]{:S(2)}) %collective-permute-start.3) | collective-permute-done | bytes 1081376 | tf_op jit(solution)/shard_map/ppermute | solution.py:295
  62.4 1.8 %add.36.refs_0_ = f32[528,512]{1,0:T(8,128)S(1)} add(f32[528,512]{1,0:T(8,128)} %get-tuple-element.54, f32[528,512]{1,0:T(8,128)} %collective-permute-done.3) | non-fusion elementwise | flops 270336 | bytes 3244032 | tf_op jit(solution)/shard_map/add | solution.py:394
  64.2 4.0 %collective-permute-done.4 = f32[560,128]{1,0:T(8,128)S(1)} collective-permute-done((f32[560,128]{1,0:T(8,128)}, f32[560,128]{1,0:T(8,128)S(1)}, u32[]{:S(2)}, u32[]{:S(2)}) %collective-permute-start.4) | collective-permute-done | bytes 286752 | tf_op jit(solution)/shard_map/ppermute | solution.py:295
  70.8 4.5 %collective-permute-start.6 = (f32[1120,128]{1,0:T(8,128)S(1)}, f32[1120,128]{1,0:T(8,128)S(1)}, u32[]{:S(2)}, u32[]{:S(2)}) collective-permute-start(f32[1120,128]{1,0:T(8,128)S(1)} %constant_dynamic-update-slice_fusion.refs_0_), channel_id=1, source_target_pairs={{0,1},{1,2},{2,3},{9,8},{10,9},{11,10},{16,17},{17,18},{18,19},{25... | collective-permute-start | bytes 1720328 | tf_op jit(solution)/shard_map/ppermute | solution.py:306
  75.4 1.8 %collective-permute-start.7 = (f32[440,128]{1,0:T(8,128)S(1)}, f32[440,128]{1,0:T(8,128)S(1)}, u32[]{:S(2)}, u32[]{:S(2)}) collective-permute-start(f32[440,128]{1,0:T(8,128)S(1)} %add_bitcast_fusion), channel_id=1, source_target_pairs={{0,16},{8,24},{16,0},{24,8},{1,17},{9,25},{17,1},{25,9},{2,18},{10... | collective-permute-start | bytes 675848 | tf_op jit(solution)/shard_map/ppermute | solution.py:295
  77.2 5.0 %embed_update.5 = (f32[16000,256]{1,0:T(8,128)}, f32[16000,256]{1,0:T(8,128)}) custom-call(s32[162]{0:T(256)S(1)} %bitcast.28, f32[1120,128]{1,0:T(8,128)S(1)} %constant_dynamic-update-slice_fusion.refs_0_, f32[64,256]{1,0:T(8,128)S(1)} %bitcast.17, f32[16000,256]{1,0:T(8,128)} %refs_7_.3, f32[16000,256]{1,0:T(8,128)} %refs_8_.3), custom_call_target="tpu_custom_call" | custom-call | tf_op jit(solution)/shard_map/embed_update/pallas_call | solution.py:197
  84.1 6.2 %collective-permute-start.9 = (f32[880,128]{1,0:T(8,128)S(1)}, f32[880,128]{1,0:T(8,128)S(1)}, u32[]{:S(2)}, u32[]{:S(2)}) collective-permute-start(f32[880,128]{1,0:T(8,128)S(1)} %constant_dynamic-update-slice_fusion.2.refs_0_), channel_id=1, source_target_pairs={{0,1},{1,2},{2,3},{9,8},{10,9},{11,10},{16,17},{17,18},{18,19},{25... | collective-permute-start | bytes 1351688 | tf_op jit(solution)/shard_map/ppermute | solution.py:306
  91.1 5.4 %embed_update.6 = (f32[16000,256]{1,0:T(8,128)}, f32[16000,256]{1,0:T(8,128)}) custom-call(s32[162]{0:T(256)S(1)} %bitcast.29, f32[1120,128]{1,0:T(8,128)S(1)} %collective-permute-done.6.refs_0_, f32[1120,128]{1,0:T(8,128)} %copy-done.6, f32[64,256]{1,0:T(8,128)S(1)} %bitcast.18, ...), custom_call_target="tpu_custom_call", output_to_operand_aliasing={{0}: (6, {}), {1}: (7, {})} | custom-call | tf_op jit(solution)/shard_map/embed_update/pallas_call | solution.py:197
  98.8 1.9 %collective-permute-start.14 = (f32[880,128]{1,0:T(8,128)S(1)}, f32[880,128]{1,0:T(8,128)S(1)}, u32[]{:S(2)}, u32[]{:S(2)}) collective-permute-start(f32[880,128]{1,0:T(8,128)S(1)} %collective-permute-done.9.refs_1_.refs_0_), channel_id=1, source_target_pairs={{0,8},{8,0},{16,24},{24,16},{1,9},{9,1},{17,25},{25,17},{2,10},{10... | collective-permute-start | bytes 1351688 | tf_op jit(solution)/shard_map/ppermute | solution.py:295
  102.9 7.6 %embed_update.7 = (f32[16000,256]{1,0:T(8,128)}, f32[16000,256]{1,0:T(8,128)}) custom-call(s32[162]{0:T(256)S(1)} %bitcast.30, f32[880,128]{1,0:T(8,128)S(1)} %constant_dynamic-update-slice_fusion.2.refs_0_, f32[880,128]{1,0:T(8,128)S(1)} %collective-permute-done.9.refs_1_.refs_0_, ...), custom_call_target="tpu_custom_call", output_to_operand_aliasing={{0}: (7, {}), {1}: (8, {})} | custom-call | tf_op jit(solution)/shard_map/embed_update/pallas_call | solution.py:197
  113.5 8.7 %embed_update.8 = (f32[16000,256]{1,0:T(8,128)}, f32[16000,256]{1,0:T(8,128)}) custom-call(s32[162]{0:T(256)S(1)} %bitcast.31, f32[1120,128]{1,0:T(8,128)S(1)} %collective-permute-done.6.refs_0_, f32[1120,128]{1,0:T(8,128)} %copy-done.6, f32[1120,128]{1,0:T(8,128)} %copy-done.13, ...), custom_call_target="tpu_custom_call", output_to_operand_aliasing={{0}: (10, {}), {1}: (11, {})} | custom-call | tf_op jit(solution)/shard_map/embed_update/pallas_call | solution.py:197
  124.7 2.5 %collective-permute-done.19.refs_3_ = f32[880,128]{1,0:T(8,128)S(1)} collective-permute-done((f32[880,128]{1,0:T(8,128)S(1)}, f32[880,128]{1,0:T(8,128)S(1)}, u32[]{:S(2)}, u32[]{:S(2)}) %collective-permute-start.19) | collective-permute-done | bytes 450592 | tf_op jit(solution)/shard_map/ppermute | solution.py:295
  128.5 7.5 %embed_update.9 = (f32[16000,256]{1,0:T(8,128)}, f32[16000,256]{1,0:T(8,128)}) custom-call(s32[162]{0:T(256)S(1)} %bitcast.32, f32[880,128]{1,0:T(8,128)S(1)} %collective-permute-done.9.refs_1_.refs_0_, f32[880,128]{1,0:T(8,128)S(1)} %copy-done.3, f32[880,128]{1,0:T(8,128)} %copy-done.17, ...), custom_call_target="tpu_custom_call", output_to_operand_aliasing={{0}: (10, {}), {1}: (11, {})} | custom-call | tf_op jit(solution)/shard_map/embed_update/pallas_call | solution.py:197
  137.5 9.3 %layer_update.1 = (f32[2112,512]{1,0:T(8,128)}, f32[2112,512]{1,0:T(8,128)}) custom-call(s32[162]{0:T(256)S(1)} %bitcast.33, f32[528,512]{1,0:T(8,128)} %copy-done.4, f32[528,512]{1,0:T(8,128)} %copy-done.9, f32[528,512]{1,0:T(8,128)} %copy-done.5, f32[528,512]{1,0:T(8,128)} %copy-done.10, f32[2112,512]{1,0:T(8,128)} %bitcast.41, f32[2112,512]{1,0:T(8,128)} %bitcast.42), custom_call_target="tpu_custom_call" | custom-call | tf_op jit(solution)/shard_map/layer_update/pallas_call | solution.py:197
  (91 shorter events, 24.1 us)
Async XLA Ops:
  7.2 51.1 %reduce-scatter.2.cloned.1.call-start = ((), (), s32[]{:S(2)}) async-start(), calls=%async_computation.2 | async-start | bytes 1433600 | tf_op jit(solution)/shard_map/reduce_scatter | solution.py:425
  13.9 3.9 %collective-permute-start = (f32[2240,128]{1,0:T(8,128)}, f32[2240,128]{1,0:T(8,128)S(1)}, u32[]{:S(2)}, u32[]{:S(2)}) collective-permute-start(f32[2240,128]{1,0:T(8,128)} %project.4), channel_id=1, source_target_pairs={{0,8},{8,0},{16,24},{24,16},{1,9},{9,1},{17,25},{25,17},{2,10},{10... | collective-permute-start | bytes 3440648 | tf_op jit(solution)/shard_map/ppermute | solution.py:295
  17.7 11.3 %collective-permute-start.1 = (f32[1056,512]{1,0:T(8,128)}, f32[1056,512]{1,0:T(8,128)S(1)}, u32[]{:S(2)}, u32[]{:S(2)}) collective-permute-start(f32[1056,512]{1,0:T(8,128)} %widen.2), channel_id=1, source_target_pairs={{0,8},{8,0},{16,24},{24,16},{1,9},{9,1},{17,25},{25,17},{2,10},{10... | collective-permute-start | bytes 6488072 | tf_op jit(solution)/shard_map/ppermute | solution.py:295
  28.4 9.0 %collective-permute-start.2 = (f32[1760,128]{1,0:T(8,128)S(1)}, f32[1760,128]{1,0:T(8,128)S(1)}, u32[]{:S(2)}, u32[]{:S(2)}) collective-permute-start(f32[1760,128]{1,0:T(8,128)S(1)} %project.6), channel_id=1, source_target_pairs={{0,8},{8,0},{16,24},{24,16},{1,9},{9,1},{17,25},{25,17},{2,10},{10... | collective-permute-start | bytes 2703368 | tf_op jit(solution)/shard_map/ppermute | solution.py:295
  34.6 27.8 %collective-permute-start.3 = (f32[528,512]{1,0:T(8,128)}, f32[528,512]{1,0:T(8,128)}, u32[]{:S(2)}, u32[]{:S(2)}) collective-permute-start(f32[528,512]{1,0:T(8,128)} %get-tuple-element.54), channel_id=1, source_target_pairs={{0,16},{8,24},{16,0},{24,8},{1,17},{9,25},{17,1},{25,9},{2,18},{10... | collective-permute-start | bytes 3244040 | tf_op jit(solution)/shard_map/ppermute | solution.py:295
  43.5 31.8 %all-to-all-start = ((f32[4,440,128]{2,1,0:T(8,128)}), f32[4,440,128]{2,1,0:T(8,128)S(1)}, u32[]{:S(2)}, u32[]{:S(2)}) async-start(f32[4,440,128]{2,1,0:T(8,128)} %bitcast.4), calls=%async_computation | async-start | bytes 1802240 | tf_op jit(solution)/shard_map/all_to_all | solution.py:427
  58.3 9.9 %collective-permute-start.4 = (f32[560,128]{1,0:T(8,128)}, f32[560,128]{1,0:T(8,128)S(1)}, u32[]{:S(2)}, u32[]{:S(2)}) collective-permute-start(f32[560,128]{1,0:T(8,128)} %bitcast.43), channel_id=1, source_target_pairs={{0,16},{8,24},{16,0},{24,8},{1,17},{9,25},{17,1},{25,9},{2,18},{10... | collective-permute-start | bytes 860168 | tf_op jit(solution)/shard_map/ppermute | solution.py:295
  69.1 1.6 %collective-permute-start.5 = (f32[560,128]{1,0:T(8,128)S(1)}, f32[560,128]{1,0:T(8,128)S(1)}, u32[]{:S(2)}, u32[]{:S(2)}) collective-permute-start(f32[560,128]{1,0:T(8,128)S(1)} %add.37), channel_id=1, source_target_pairs={{0,8},{8,0},{16,24},{24,16},{1,9},{9,1},{17,25},{25,17},{2,10},{10... | collective-permute-start | bytes 860168 | tf_op jit(solution)/shard_map/ppermute | solution.py:295
  70.8 11.7 %collective-permute-start.6 = (f32[1120,128]{1,0:T(8,128)S(1)}, f32[1120,128]{1,0:T(8,128)S(1)}, u32[]{:S(2)}, u32[]{:S(2)}) collective-permute-start(f32[1120,128]{1,0:T(8,128)S(1)} %constant_dynamic-update-slice_fusion.refs_0_), channel_id=1, source_target_pairs={{0,1},{1,2},{2,3},{9,8},{10,9},{11,10},{16,17},{17,18},{18,19},{25... | collective-permute-start | bytes 1720328 | tf_op jit(solution)/shard_map/ppermute | solution.py:306
  75.4 7.1 %collective-permute-start.7 = (f32[440,128]{1,0:T(8,128)S(1)}, f32[440,128]{1,0:T(8,128)S(1)}, u32[]{:S(2)}, u32[]{:S(2)}) collective-permute-start(f32[440,128]{1,0:T(8,128)S(1)} %add_bitcast_fusion), channel_id=1, source_target_pairs={{0,16},{8,24},{16,0},{24,8},{1,17},{9,25},{17,1},{25,9},{2,18},{10... | collective-permute-start | bytes 675848 | tf_op jit(solution)/shard_map/ppermute | solution.py:295
  82.6 7.7 %collective-permute-start.11 = (f32[1120,128]{1,0:T(8,128)S(1)}, f32[1120,128]{1,0:T(8,128)S(1)}, u32[]{:S(2)}, u32[]{:S(2)}) collective-permute-start(f32[1120,128]{1,0:T(8,128)S(1)} %collective-permute-done.6.refs_0_), channel_id=1, source_target_pairs={{0,8},{8,0},{16,24},{24,16},{1,9},{9,1},{17,25},{25,17},{2,10},{10... | collective-permute-start | bytes 1720328 | tf_op jit(solution)/shard_map/ppermute | solution.py:295
  83.1 13.4 %collective-permute-start.10 = (f32[1120,128]{1,0:T(8,128)S(1)}, f32[1120,128]{1,0:T(8,128)S(1)}, u32[]{:S(2)}, u32[]{:S(2)}) collective-permute-start(f32[1120,128]{1,0:T(8,128)S(1)} %collective-permute-done.6.refs_0_), channel_id=1, source_target_pairs={{1,2},{2,3},{9,8},{10,9},{17,18},{18,19},{25,24},{26,25},{5,6},{6,... | collective-permute-start | bytes 1720328 | tf_op jit(solution)/shard_map/ppermute | solution.py:306
  84.1 13.1 %collective-permute-start.9 = (f32[880,128]{1,0:T(8,128)S(1)}, f32[880,128]{1,0:T(8,128)S(1)}, u32[]{:S(2)}, u32[]{:S(2)}) collective-permute-start(f32[880,128]{1,0:T(8,128)S(1)} %constant_dynamic-update-slice_fusion.2.refs_0_), channel_id=1, source_target_pairs={{0,1},{1,2},{2,3},{9,8},{10,9},{11,10},{16,17},{17,18},{18,19},{25... | collective-permute-start | bytes 1351688 | tf_op jit(solution)/shard_map/ppermute | solution.py:306
  96.5 14.0 %collective-permute-start.13 = (f32[1120,128]{1,0:T(8,128)S(1)}, f32[1120,128]{1,0:T(8,128)S(1)}, u32[]{:S(2)}, u32[]{:S(2)}) collective-permute-start(f32[1120,128]{1,0:T(8,128)S(1)} %collective-permute-done.10.refs_2_), channel_id=1, source_target_pairs={{2,3},{9,8},{18,19},{25,24},{6,7},{13,12},{22,23},{29,28}} | collective-permute-start | bytes 1720328 | tf_op jit(solution)/shard_map/ppermute | solution.py:306
  97.2 25.9 %collective-permute-start.18 = (f32[528,512]{1,0:T(8,128)S(1)}, f32[528,512]{1,0:T(8,128)S(1)}, u32[]{:S(2)}, u32[]{:S(2)}) collective-permute-start(f32[528,512]{1,0:T(8,128)S(1)} %copy-done.11), channel_id=1, source_target_pairs={{0,16},{8,24},{16,0},{24,8},{1,17},{9,25},{17,1},{25,9},{2,18},{10... | collective-permute-start | bytes 3244040 | tf_op jit(solution)/shard_map/ppermute | solution.py:295
  98.8 3.3 %collective-permute-start.14 = (f32[880,128]{1,0:T(8,128)S(1)}, f32[880,128]{1,0:T(8,128)S(1)}, u32[]{:S(2)}, u32[]{:S(2)}) collective-permute-start(f32[880,128]{1,0:T(8,128)S(1)} %collective-permute-done.9.refs_1_.refs_0_), channel_id=1, source_target_pairs={{0,8},{8,0},{16,24},{24,16},{1,9},{9,1},{17,25},{25,17},{2,10},{10... | collective-permute-start | bytes 1351688 | tf_op jit(solution)/shard_map/ppermute | solution.py:295
  100.7 9.9 %collective-permute-start.12 = (f32[880,128]{1,0:T(8,128)S(1)}, f32[880,128]{1,0:T(8,128)S(1)}, u32[]{:S(2)}, u32[]{:S(2)}) collective-permute-start(f32[880,128]{1,0:T(8,128)S(1)} %collective-permute-done.9.refs_1_.refs_0_), channel_id=1, source_target_pairs={{1,2},{2,3},{9,8},{10,9},{17,18},{18,19},{25,24},{26,25},{5,6},{6,... | collective-permute-start | bytes 1351688 | tf_op jit(solution)/shard_map/ppermute | solution.py:306
  101.4 11.1 %collective-permute-start.16 = (f32[1120,128]{1,0:T(8,128)S(1)}, f32[1120,128]{1,0:T(8,128)S(1)}, u32[]{:S(2)}, u32[]{:S(2)}) collective-permute-start(f32[1120,128]{1,0:T(8,128)S(1)} %collective-permute-done.10.refs_2_), channel_id=1, source_target_pairs={{0,8},{8,0},{16,24},{24,16},{1,9},{9,1},{17,25},{25,17},{2,10},{10... | collective-permute-start | bytes 1720328 | tf_op jit(solution)/shard_map/ppermute | solution.py:295
  110.5 2.0 %collective-permute-start.17 = (f32[1120,128]{1,0:T(8,128)S(1)}, f32[1120,128]{1,0:T(8,128)S(1)}, u32[]{:S(2)}, u32[]{:S(2)}) collective-permute-start(f32[1120,128]{1,0:T(8,128)S(1)} %collective-permute-done.13.refs_4_), channel_id=1, source_target_pairs={{0,8},{8,0},{16,24},{24,16},{1,9},{9,1},{17,25},{25,17},{2,10},{10... | collective-permute-start | bytes 1720328 | tf_op jit(solution)/shard_map/ppermute | solution.py:295
  110.6 11.6 %collective-permute-start.15 = (f32[880,128]{1,0:T(8,128)S(1)}, f32[880,128]{1,0:T(8,128)S(1)}, u32[]{:S(2)}, u32[]{:S(2)}) collective-permute-start(f32[880,128]{1,0:T(8,128)S(1)} %collective-permute-done.12.refs_2_), channel_id=1, source_target_pairs={{2,3},{9,8},{18,19},{25,24},{6,7},{13,12},{22,23},{29,28}} | collective-permute-start | bytes 1351688 | tf_op jit(solution)/shard_map/ppermute | solution.py:306
  111.3 24.8 %collective-permute-start.21 = (f32[528,512]{1,0:T(8,128)S(1)}, f32[528,512]{1,0:T(8,128)S(1)}, u32[]{:S(2)}, u32[]{:S(2)}) collective-permute-start(f32[528,512]{1,0:T(8,128)S(1)} %add.36.refs_0_), channel_id=1, source_target_pairs={{0,8},{8,0},{16,24},{24,16},{1,9},{9,1},{17,25},{25,17},{2,10},{10... | collective-permute-start | bytes 3244040 | tf_op jit(solution)/shard_map/ppermute | solution.py:295
  123.3 12.8 %collective-permute-start.22 = (f32[528,512]{1,0:T(8,128)S(1)}, f32[528,512]{1,0:T(8,128)S(1)}, u32[]{:S(2)}, u32[]{:S(2)}) collective-permute-start(f32[528,512]{1,0:T(8,128)S(1)} %add.43.refs_2_), channel_id=1, source_target_pairs={{0,8},{8,0},{16,24},{24,16},{1,9},{9,1},{17,25},{25,17},{2,10},{10... | collective-permute-start | bytes 3244040 | tf_op jit(solution)/shard_map/ppermute | solution.py:295
  124.1 3.0 %collective-permute-start.19 = (f32[880,128]{1,0:T(8,128)S(1)}, f32[880,128]{1,0:T(8,128)S(1)}, u32[]{:S(2)}, u32[]{:S(2)}) collective-permute-start(f32[880,128]{1,0:T(8,128)S(1)} %collective-permute-done.12.refs_2_), channel_id=1, source_target_pairs={{0,8},{8,0},{16,24},{24,16},{1,9},{9,1},{17,25},{25,17},{2,10},{10... | collective-permute-start | bytes 1351688 | tf_op jit(solution)/shard_map/ppermute | solution.py:295
  124.2 3.5 %collective-permute-start.20 = (f32[880,128]{1,0:T(8,128)S(1)}, f32[880,128]{1,0:T(8,128)S(1)}, u32[]{:S(2)}, u32[]{:S(2)}) collective-permute-start(f32[880,128]{1,0:T(8,128)S(1)} %collective-permute-done.15.refs_4_), channel_id=1, source_target_pairs={{0,8},{8,0},{16,24},{24,16},{1,9},{9,1},{17,25},{25,17},{2,10},{10... | collective-permute-start | bytes 1351688 | tf_op jit(solution)/shard_map/ppermute | solution.py:295
  (22 other events, 136.1 us)
Sparse Core Ops, SparseCore 0:
  24.8 33.3 reduce-scatter.1

commit v3 on v2

--- a/solution.py
+++ b/solution.py
@@ -376,14 +376,16 @@
     l_keep = table.add(lambda g, z: [core(g) * units])
 
 
-    def l_entry(g, z):
-        parts = []
-        for n, (f, size) in enumerate(zip(firsts, pieces)):
-            for h in (0, 1):
-                parts += [((core(g) ^ h) * units + f + u, 2 * n + h, u) for u in range(size)]
-        return [1] * len(parts) + [p for column in zip(*parts) for p in column]
-
-    l_all = table.add(l_entry)
+    def l_place(n):
+        def entry(g, z):
+            parts = [
+                ((core(g) ^ h) * units + firsts[n] + u, h, u) for h in (0, 1) for u in range(pieces[n])
+            ]
+            return [1] * len(parts) + [p for column in zip(*parts) for p in column]
+
+        return table.add(entry)
+
+    l_place_of = [l_place(n) for n in range(len(pieces))]
     tab = table.mine()
     order = Order()
 
@@ -411,9 +413,11 @@
         l_total[n] = add(chip[n], l_got[n])
         l_other[n] = swap_groups(l_total[n], 1)
 
-    def layer_finish():
-        sources = [x for pair in zip(l_total, l_other) for x in pair]
-        state["layer"] = run(layer_update, l_all, 2 * units, sources, weights, momentum, groups, state["layer"])
+    def layer_finish(n):
+        sources = (l_total[n], l_other[n])
+        state["layer"] = run(
+            layer_update, l_place_of[n], 2 * pieces[n], sources, weights, momentum, groups, state["layer"]
+        )
 
     def project_send(c):
         sent[c] = swap_groups(run(project, p_send[c], 4, tiles[c], *embed), 1)
@@ -421,15 +425,11 @@
     def project_keep(c):
         chip = run(project, p_keep[c], 4, tiles[c], *embed, sent[c])
         chip = chip.reshape((4, -1) + chip.shape[1:])
-        if c == 0:
-            kept[c] = lax.psum_scatter(chip, "tensor", scatter_dimension=0)
-        else:
-            kept[c] = lax.all_to_all(chip, "tensor", 0, 0)
+        kept[c] = lax.all_to_all(chip, "tensor", 0, 0)
 
     def far_send(c):
         kept[c] = wait(kept[c])
-        if c == 1:
-            kept[c] = order.done((kept[c][0] + kept[c][1]) + (kept[c][2] + kept[c][3]))
+        kept[c] = order.done((kept[c][0] + kept[c][1]) + (kept[c][2] + kept[c][3]))
         kept[c] = kept[c].reshape(-1, kept[c].shape[-1])
         summed[c] = swap_groups(kept[c], 2)
 
@@ -469,6 +469,7 @@
     spread(0)
     far_send(1)
     finish(0, own, 2, whole_block[0])
+    layer_finish(0)
     step(0, 0)
     far_sum(1)
     spread(1)
@@ -483,7 +484,7 @@
     step(1, 2)
     layer_sum(1)
     finish(1, far, 4, *received(1, 3))
-    layer_finish()
+    layer_finish(1)
     new_layer, new_layer_momentum = (x.reshape(global_layer.shape) for x in state["layer"])
     return (new_layer, new_layer_momentum, *state["embed"])
 

time: 155 us -> 150 us (0.968)
  between operations: 14.5 us -> 1.27 us
  waiting for transfers between devices: 21.8 us -> 31.1 us
  Pallas kernels: 71 us -> 72.8 us
    all_to_all x1 -> x2, waiting for transfers between devices: 0.01 us -> 17.8 us  [project_keep(): kept[c] = lax.all_to_all(chip, 'tensor', 0, 0)]
    reduce_scatter x1 -> x0, waiting for transfers between devices: 9.87 us -> none  [project_keep(): kept[c] = lax.psum_scatter(chip, 'tensor', scatter_dimension=0)]
    all_to_all x1 -> x2, starting transfers between devices: 4.85 us -> 9.84 us  [project_keep(): kept[c] = lax.all_to_all(chip, 'tensor', 0, 0)]
    ppermute x6, starting transfers between devices: 13.4 us -> 9.86 us  [shift(): return lax.ppermute(x, ('groups', 'tensor'), pairs)]
    ppermute x17, starting transfers between devices: 15.5 us -> 12.8 us  [swap_groups(): return lax.ppermute(x, 'groups', [(g, g ^ bit) for g in range(4)])]
    pallas_call x6 -> x7, Pallas kernels: 43.5 us -> 45.3 us  [update(): pl.pallas_call(functools.partial(update_kernel, at, unit, sub, subs, dept...]
    ppermute x17, waiting for transfers between devices: 11.6 us -> 13.3 us  [swap_groups(): return lax.ppermute(x, 'groups', [(g, g ^ bit) for g in range(4)])]
    unnamed x44 -> x42, local copies, waits for them, and re-layouts: 8.81 us -> 8.29 us
  transfers between devices with their start and end apart: 25 -> 25, of which waited for: 11 -> 10; matrix products, arithmetic and copies ran while one was open for 2% -> 1% of each run, Pallas kernels for 37% -> 42%
where the time goes in v3:
time: 150 us; the launch traced here: 149 us
  Pallas kernels  72.8 us (49%)
  starting transfers between devices  32.5 us (22%)
  waiting for transfers between devices  31.1 us (21%)
  local copies, waits for them, and re-layouts  9.03 us (6%)
  other arithmetic  2.16 us (1%)
    pallas_call x7, Pallas kernels, update(): pl.pallas_call(functools.partial(update_kernel, at, unit, sub, subs, dept...  45.3 us
    pallas_call x4, Pallas kernels, project(): pl.pallas_call(functools.partial(project_kernel, at, count, tile), in_spe...  19.9 us
    all_to_all x2, waiting for transfers between devices, project_keep(): kept[c] = lax.all_to_all(chip, 'tensor', 0, 0)  17.8 us
    ppermute x17, waiting for transfers between devices, swap_groups(): return lax.ppermute(x, 'groups', [(g, g ^ bit) for g in range(4)])  13.3 us
    ppermute x17, starting transfers between devices, swap_groups(): return lax.ppermute(x, 'groups', [(g, g ^ bit) for g in range(4)])  12.8 us
    ppermute x6, starting transfers between devices, shift(): return lax.ppermute(x, ('groups', 'tensor'), pairs)  9.86 us
    all_to_all x2, starting transfers between devices, project_keep(): kept[c] = lax.all_to_all(chip, 'tensor', 0, 0)  9.84 us
    unnamed x42, local copies, waits for them, and re-layouts  8.29 us
  transfers between devices with their start and end apart: 25, of which 10 were waited for; matrix products, arithmetic and copies ran while one was open for 1% of the time, Pallas kernels for 42%

profile of v3, /device:TPU:0, one launch (start us, length us, event | category | flops | bytes accessed | tf_op | source)
XLA Modules:
  0.0 148.8 jit_solution(8198527407680772475)
XLA Ops:
  2.2 5.1 %project.4 = f32[2240,128]{1,0:T(8,128)} custom-call(s32[162]{0:T(256)S(1)} %bitcast.23, f32[16000,256]{1,0:T(8,128)} %refs_7_.3, bf16[16000,256]{1,0:T(8,128)(2,1)} %bitcast.36, f32[64,256]{1,0:T(8,128)S(1)} %bitcast.14), custom_call_target="tpu_custom_call" | custom-call | tf_op jit(solution)/shard_map/project/pallas_call | solution.py:98
  7.8 3.3 %widen.2 = f32[1056,512]{1,0:T(8,128)} custom-call(s32[162]{0:T(256)S(1)} %bitcast.24, bf16[2112,512]{1,0:T(8,128)(2,1)} %bitcast.44), custom_call_target="tpu_custom_call" | custom-call | tf_op jit(solution)/shard_map/widen/pallas_call | solution.py:268
  12.3 5.8 %project.5 = f32[2240,128]{1,0:T(8,128)} custom-call(s32[162]{0:T(256)S(1)} %bitcast.25, f32[16000,256]{1,0:T(8,128)} %refs_7_.3, bf16[16000,256]{1,0:T(8,128)(2,1)} %bitcast.37, f32[64,256]{1,0:T(8,128)S(1)} %bitcast.15, f32[2240,128]{1,0:T(8,128)} %copy-done.8), custom_call_target="tpu_custom_call" | custom-call | tf_op jit(solution)/shard_map/project/pallas_call | solution.py:98
  18.1 6.3 %all-to-all-start.1 = ((f32[4,560,128]{2,1,0:T(8,128)}), f32[4,560,128]{2,1,0:T(8,128)S(1)}, u32[]{:S(2)}, u32[]{:S(2)}) async-start(f32[4,560,128]{2,1,0:T(8,128)} %bitcast.46), calls=%async_computation.1 | async-start | bytes 2293760 | tf_op jit(solution)/shard_map/all_to_all | solution.py:428
  24.4 3.7 %project.6 = f32[1760,128]{1,0:T(8,128)S(1)} custom-call(s32[162]{0:T(256)S(1)} %bitcast.26, f32[16000,256]{1,0:T(8,128)} %refs_7_.3, bf16[16000,256]{1,0:T(8,128)(2,1)} %bitcast.38, f32[64,256]{1,0:T(8,128)S(1)} %bitcast.16), custom_call_target="tpu_custom_call" | custom-call | tf_op jit(solution)/shard_map/project/pallas_call | solution.py:98
  29.5 4.3 %widen.3 = (f32[528,512]{1,0:T(8,128)}, f32[528,512]{1,0:T(8,128)}) custom-call(s32[162]{0:T(256)S(1)} %bitcast.27, bf16[2112,512]{1,0:T(8,128)(2,1)} %bitcast.45, f32[1056,512]{1,0:T(8,128)} %copy-done.7), custom_call_target="tpu_custom_call" | custom-call | tf_op jit(solution)/shard_map/widen/pallas_call | solution.py:268
  36.4 5.3 %project.7 = f32[1760,128]{1,0:T(8,128)} custom-call(s32[162]{0:T(256)S(1)} %bitcast.28, f32[16000,256]{1,0:T(8,128)} %refs_7_.3, bf16[16000,256]{1,0:T(8,128)(2,1)} %bitcast.39, f32[64,256]{1,0:T(8,128)S(1)} %bitcast.17, f32[1760,128]{1,0:T(8,128)} %copy-done.11), custom_call_target="tpu_custom_call" | custom-call | tf_op jit(solution)/shard_map/project/pallas_call | solution.py:98
  41.6 10.8 %all-to-all-done.1 = f32[4,560,128]{2,1,0:T(8,128)S(1)} async-done(((f32[4,560,128]{2,1,0:T(8,128)}), f32[4,560,128]{2,1,0:T(8,128)S(1)}, u32[]{:S(2)}, u32[]{:S(2)}) %all-to-all-start.1) | async-done | bytes 1146912 | tf_op jit(solution)/shard_map/all_to_all | solution.py:428
  52.5 3.5 %all-to-all-start = ((f32[4,440,128]{2,1,0:T(8,128)}), f32[4,440,128]{2,1,0:T(8,128)S(1)}, u32[]{:S(2)}, u32[]{:S(2)}) async-start(f32[4,440,128]{2,1,0:T(8,128)} %bitcast.4), calls=%async_computation | async-start | bytes 1802240 | tf_op jit(solution)/shard_map/all_to_all | solution.py:428
  57.6 3.3 %collective-permute-done.3 = f32[528,512]{1,0:T(8,128)} collective-permute-done((f32[528,512]{1,0:T(8,128)}, f32[528,512]{1,0:T(8,128)}, u32[]{:S(2)}, u32[]{:S(2)}) %collective-permute-start.3) | collective-permute-done | bytes 1081376 | tf_op jit(solution)/shard_map/ppermute | solution.py:295
  60.9 1.8 %add.52.refs_0_ = f32[528,512]{1,0:T(8,128)S(1)} add(f32[528,512]{1,0:T(8,128)} %get-tuple-element.57, f32[528,512]{1,0:T(8,128)} %collective-permute-done.3) | non-fusion elementwise | flops 270336 | bytes 3244032 | tf_op jit(solution)/shard_map/add | solution.py:396
  62.8 3.8 %collective-permute-done.4 = f32[560,128]{1,0:T(8,128)S(1)} collective-permute-done((f32[560,128]{1,0:T(8,128)S(1)}, f32[560,128]{1,0:T(8,128)S(1)}, u32[]{:S(2)}, u32[]{:S(2)}) %collective-permute-start.4) | collective-permute-done | bytes 286752 | tf_op jit(solution)/shard_map/ppermute | solution.py:295
  68.2 4.0 %collective-permute-start.6 = (f32[1120,128]{1,0:T(8,128)S(1)}, f32[1120,128]{1,0:T(8,128)S(1)}, u32[]{:S(2)}, u32[]{:S(2)}) collective-permute-start(f32[1120,128]{1,0:T(8,128)S(1)} %constant_dynamic-update-slice_fusion.refs_0_), channel_id=1, source_target_pairs={{0,1},{1,2},{2,3},{9,8},{10,9},{11,10},{16,17},{17,18},{18,19},{25... | collective-permute-start | bytes 1720328 | tf_op jit(solution)/shard_map/ppermute | solution.py:306
  72.2 6.9 %all-to-all-done = f32[4,440,128]{2,1,0:T(8,128)S(1)} async-done(((f32[4,440,128]{2,1,0:T(8,128)}), f32[4,440,128]{2,1,0:T(8,128)S(1)}, u32[]{:S(2)}, u32[]{:S(2)}) %all-to-all-start) | async-done | bytes 901152 | tf_op jit(solution)/shard_map/all_to_all | solution.py:428
  80.8 5.0 %embed_update.5 = (f32[16000,256]{1,0:T(8,128)}, f32[16000,256]{1,0:T(8,128)}) custom-call(s32[162]{0:T(256)S(1)} %bitcast.29, f32[1120,128]{1,0:T(8,128)S(1)} %constant_dynamic-update-slice_fusion.refs_0_, f32[64,256]{1,0:T(8,128)S(1)} %bitcast.18, f32[16000,256]{1,0:T(8,128)} %refs_7_.3, f32[16000,256]{1,0:T(8,128)} %refs_8_.3), custom_call_target="tpu_custom_call" | custom-call | tf_op jit(solution)/shard_map/embed_update/pallas_call | solution.py:197
  85.8 5.6 %layer_update.2 = (f32[2112,512]{1,0:T(8,128)}, f32[2112,512]{1,0:T(8,128)}) custom-call(s32[162]{0:T(256)S(1)} %bitcast.30, f32[528,512]{1,0:T(8,128)} %copy-done.5, f32[528,512]{1,0:T(8,128)} %collective-permute-done.7.refs_1_, f32[2112,512]{1,0:T(8,128)} %bitcast.40, f32[2112,512]{1,0:T(8,128)} %bitcast.42), custom_call_target="tpu_custom_call" | custom-call | tf_op jit(solution)/shard_map/layer_update/pallas_call | solution.py:197
  93.0 3.1 %collective-permute-start.10 = (f32[880,128]{1,0:T(8,128)S(1)}, f32[880,128]{1,0:T(8,128)S(1)}, u32[]{:S(2)}, u32[]{:S(2)}) collective-permute-start(f32[880,128]{1,0:T(8,128)S(1)} %constant_dynamic-update-slice_fusion.2.refs_0_), channel_id=1, source_target_pairs={{0,1},{1,2},{2,3},{9,8},{10,9},{11,10},{16,17},{17,18},{18,19},{25... | collective-permute-start | bytes 1351688 | tf_op jit(solution)/shard_map/ppermute | solution.py:306
  97.0 5.2 %embed_update.6 = (f32[16000,256]{1,0:T(8,128)}, f32[16000,256]{1,0:T(8,128)}) custom-call(s32[162]{0:T(256)S(1)} %bitcast.31, f32[1120,128]{1,0:T(8,128)S(1)} %collective-permute-done.6.refs_0_, f32[1120,128]{1,0:T(8,128)} %copy-done.6, f32[64,256]{1,0:T(8,128)S(1)} %bitcast.19, ...), custom_call_target="tpu_custom_call", output_to_operand_aliasing={{0}: (6, {}), {1}: (7, {})} | custom-call | tf_op jit(solution)/shard_map/embed_update/pallas_call | solution.py:197
  103.6 4.4 %collective-permute-start.15 = (f32[880,128]{1,0:T(8,128)S(1)}, f32[880,128]{1,0:T(8,128)S(1)}, u32[]{:S(2)}, u32[]{:S(2)}) collective-permute-start(f32[880,128]{1,0:T(8,128)S(1)} %collective-permute-done.10.refs_1_.refs_0_), channel_id=1, source_target_pairs={{0,8},{8,0},{16,24},{24,16},{1,9},{9,1},{17,25},{25,17},{2,10},{10... | collective-permute-start | bytes 1351688 | tf_op jit(solution)/shard_map/ppermute | solution.py:295
  110.1 7.6 %embed_update.7 = (f32[16000,256]{1,0:T(8,128)}, f32[16000,256]{1,0:T(8,128)}) custom-call(s32[162]{0:T(256)S(1)} %bitcast.32, f32[880,128]{1,0:T(8,128)S(1)} %constant_dynamic-update-slice_fusion.2.refs_0_, f32[880,128]{1,0:T(8,128)S(1)} %collective-permute-done.10.refs_1_.refs_0_, ...), custom_call_target="tpu_custom_call", output_to_operand_aliasing={{0}: (7, {}), {1}: (8, {})} | custom-call | tf_op jit(solution)/shard_map/embed_update/pallas_call | solution.py:197
  120.6 8.7 %embed_update.8 = (f32[16000,256]{1,0:T(8,128)}, f32[16000,256]{1,0:T(8,128)}) custom-call(s32[162]{0:T(256)S(1)} %bitcast.33, f32[1120,128]{1,0:T(8,128)S(1)} %collective-permute-done.6.refs_0_, f32[1120,128]{1,0:T(8,128)} %copy-done.6, f32[1120,128]{1,0:T(8,128)} %copy-done.12, ...), custom_call_target="tpu_custom_call", output_to_operand_aliasing={{0}: (10, {}), {1}: (11, {})} | custom-call | tf_op jit(solution)/shard_map/embed_update/pallas_call | solution.py:197
  130.6 2.5 %collective-permute-done.20.refs_3_ = f32[880,128]{1,0:T(8,128)S(1)} collective-permute-done((f32[880,128]{1,0:T(8,128)S(1)}, f32[880,128]{1,0:T(8,128)S(1)}, u32[]{:S(2)}, u32[]{:S(2)}) %collective-permute-start.20) | collective-permute-done | bytes 450592 | tf_op jit(solution)/shard_map/ppermute | solution.py:295
  134.5 7.5 %embed_update.9 = (f32[16000,256]{1,0:T(8,128)}, f32[16000,256]{1,0:T(8,128)}) custom-call(s32[162]{0:T(256)S(1)} %bitcast.34, f32[880,128]{1,0:T(8,128)S(1)} %collective-permute-done.10.refs_1_.refs_0_, f32[880,128]{1,0:T(8,128)S(1)} %copy-done.3, f32[880,128]{1,0:T(8,128)} %copy-done.16, ...), custom_call_target="tpu_custom_call", output_to_operand_aliasing={{0}: (10, {}), {1}: (11, {})} | custom-call | tf_op jit(solution)/shard_map/embed_update/pallas_call | solution.py:197
  143.0 5.6 %layer_update.3 = (f32[2112,512]{1,0:T(8,128)}, f32[2112,512]{1,0:T(8,128)}) custom-call(s32[162]{0:T(256)S(1)} %bitcast.35, f32[528,512]{1,0:T(8,128)} %copy-done.4, f32[528,512]{1,0:T(8,128)} %copy-done.9, f32[2112,512]{1,0:T(8,128)} %bitcast.41, f32[2112,512]{1,0:T(8,128)} %bitcast.43, ...), custom_call_target="tpu_custom_call", output_to_operand_aliasing={{0}: (5, {}), {1}: (6, {})} | custom-call | tf_op jit(solution)/shard_map/layer_update/pallas_call | solution.py:197
  (90 shorter events, 24.4 us)
Async XLA Ops:
  7.3 3.9 %collective-permute-start = (f32[2240,128]{1,0:T(8,128)}, f32[2240,128]{1,0:T(8,128)S(1)}, u32[]{:S(2)}, u32[]{:S(2)}) collective-permute-start(f32[2240,128]{1,0:T(8,128)} %project.4), channel_id=1, source_target_pairs={{0,8},{8,0},{16,24},{24,16},{1,9},{9,1},{17,25},{25,17},{2,10},{10... | collective-permute-start | bytes 3440648 | tf_op jit(solution)/shard_map/ppermute | solution.py:295
  11.1 17.1 %collective-permute-start.1 = (f32[1056,512]{1,0:T(8,128)}, f32[1056,512]{1,0:T(8,128)S(1)}, u32[]{:S(2)}, u32[]{:S(2)}) collective-permute-start(f32[1056,512]{1,0:T(8,128)} %widen.2), channel_id=1, source_target_pairs={{0,8},{8,0},{16,24},{24,16},{1,9},{9,1},{17,25},{25,17},{2,10},{10... | collective-permute-start | bytes 6488072 | tf_op jit(solution)/shard_map/ppermute | solution.py:295
  18.1 34.4 %all-to-all-start.1 = ((f32[4,560,128]{2,1,0:T(8,128)}), f32[4,560,128]{2,1,0:T(8,128)S(1)}, u32[]{:S(2)}, u32[]{:S(2)}) async-start(f32[4,560,128]{2,1,0:T(8,128)} %bitcast.46), calls=%async_computation.1 | async-start | bytes 2293760 | tf_op jit(solution)/shard_map/all_to_all | solution.py:428
  28.1 7.3 %collective-permute-start.2 = (f32[1760,128]{1,0:T(8,128)S(1)}, f32[1760,128]{1,0:T(8,128)S(1)}, u32[]{:S(2)}, u32[]{:S(2)}) collective-permute-start(f32[1760,128]{1,0:T(8,128)S(1)} %project.6), channel_id=1, source_target_pairs={{0,8},{8,0},{16,24},{24,16},{1,9},{9,1},{17,25},{25,17},{2,10},{10... | collective-permute-start | bytes 2703368 | tf_op jit(solution)/shard_map/ppermute | solution.py:295
  33.9 27.0 %collective-permute-start.3 = (f32[528,512]{1,0:T(8,128)}, f32[528,512]{1,0:T(8,128)}, u32[]{:S(2)}, u32[]{:S(2)}) collective-permute-start(f32[528,512]{1,0:T(8,128)} %get-tuple-element.57), channel_id=1, source_target_pairs={{0,16},{8,24},{16,0},{24,8},{1,17},{9,25},{17,1},{25,9},{2,18},{10... | collective-permute-start | bytes 3244040 | tf_op jit(solution)/shard_map/ppermute | solution.py:295
  52.5 26.7 %all-to-all-start = ((f32[4,440,128]{2,1,0:T(8,128)}), f32[4,440,128]{2,1,0:T(8,128)S(1)}, u32[]{:S(2)}, u32[]{:S(2)}) async-start(f32[4,440,128]{2,1,0:T(8,128)} %bitcast.4), calls=%async_computation | async-start | bytes 1802240 | tf_op jit(solution)/shard_map/all_to_all | solution.py:428
  56.0 10.5 %collective-permute-start.4 = (f32[560,128]{1,0:T(8,128)S(1)}, f32[560,128]{1,0:T(8,128)S(1)}, u32[]{:S(2)}, u32[]{:S(2)}) collective-permute-start(f32[560,128]{1,0:T(8,128)S(1)} %add_bitcast_fusion), channel_id=1, source_target_pairs={{0,16},{8,24},{16,0},{24,8},{1,17},{9,25},{17,1},{25,9},{2,18},{10... | collective-permute-start | bytes 860168 | tf_op jit(solution)/shard_map/ppermute | solution.py:295
  62.7 23.1 %collective-permute-start.7 = (f32[528,512]{1,0:T(8,128)S(1)}, f32[528,512]{1,0:T(8,128)}, u32[]{:S(2)}, u32[]{:S(2)}) collective-permute-start(f32[528,512]{1,0:T(8,128)S(1)} %add.52.refs_0_), channel_id=1, source_target_pairs={{0,8},{8,0},{16,24},{24,16},{1,9},{9,1},{17,25},{25,17},{2,10},{10... | collective-permute-start | bytes 3244040 | tf_op jit(solution)/shard_map/ppermute | solution.py:295
  66.6 1.6 %collective-permute-start.5 = (f32[560,128]{1,0:T(8,128)S(1)}, f32[560,128]{1,0:T(8,128)S(1)}, u32[]{:S(2)}, u32[]{:S(2)}) collective-permute-start(f32[560,128]{1,0:T(8,128)S(1)} %add.53), channel_id=1, source_target_pairs={{0,8},{8,0},{16,24},{24,16},{1,9},{9,1},{17,25},{25,17},{2,10},{10... | collective-permute-start | bytes 860168 | tf_op jit(solution)/shard_map/ppermute | solution.py:295
  68.2 23.2 %collective-permute-start.6 = (f32[1120,128]{1,0:T(8,128)S(1)}, f32[1120,128]{1,0:T(8,128)S(1)}, u32[]{:S(2)}, u32[]{:S(2)}) collective-permute-start(f32[1120,128]{1,0:T(8,128)S(1)} %constant_dynamic-update-slice_fusion.refs_0_), channel_id=1, source_target_pairs={{0,1},{1,2},{2,3},{9,8},{10,9},{11,10},{16,17},{17,18},{18,19},{25... | collective-permute-start | bytes 1720328 | tf_op jit(solution)/shard_map/ppermute | solution.py:306
  79.2 12.2 %collective-permute-start.8 = (f32[440,128]{1,0:T(8,128)S(1)}, f32[440,128]{1,0:T(8,128)S(1)}, u32[]{:S(2)}, u32[]{:S(2)}) collective-permute-start(f32[440,128]{1,0:T(8,128)S(1)} %add_bitcast_fusion.1), channel_id=1, source_target_pairs={{0,16},{8,24},{16,0},{24,8},{1,17},{9,25},{17,1},{25,9},{2,18},{10... | collective-permute-start | bytes 675848 | tf_op jit(solution)/shard_map/ppermute | solution.py:295
  91.6 4.6 %collective-permute-start.12 = (f32[1120,128]{1,0:T(8,128)S(1)}, f32[1120,128]{1,0:T(8,128)S(1)}, u32[]{:S(2)}, u32[]{:S(2)}) collective-permute-start(f32[1120,128]{1,0:T(8,128)S(1)} %collective-permute-done.6.refs_0_), channel_id=1, source_target_pairs={{0,8},{8,0},{16,24},{24,16},{1,9},{9,1},{17,25},{25,17},{2,10},{10... | collective-permute-start | bytes 1720328 | tf_op jit(solution)/shard_map/ppermute | solution.py:295
  92.1 10.2 %collective-permute-start.11 = (f32[1120,128]{1,0:T(8,128)S(1)}, f32[1120,128]{1,0:T(8,128)S(1)}, u32[]{:S(2)}, u32[]{:S(2)}) collective-permute-start(f32[1120,128]{1,0:T(8,128)S(1)} %collective-permute-done.6.refs_0_), channel_id=1, source_target_pairs={{1,2},{2,3},{9,8},{10,9},{17,18},{18,19},{25,24},{26,25},{5,6},{6,... | collective-permute-start | bytes 1720328 | tf_op jit(solution)/shard_map/ppermute | solution.py:306
  93.0 9.9 %collective-permute-start.10 = (f32[880,128]{1,0:T(8,128)S(1)}, f32[880,128]{1,0:T(8,128)S(1)}, u32[]{:S(2)}, u32[]{:S(2)}) collective-permute-start(f32[880,128]{1,0:T(8,128)S(1)} %constant_dynamic-update-slice_fusion.2.refs_0_), channel_id=1, source_target_pairs={{0,1},{1,2},{2,3},{9,8},{10,9},{11,10},{16,17},{17,18},{18,19},{25... | collective-permute-start | bytes 1351688 | tf_op jit(solution)/shard_map/ppermute | solution.py:306
  102.3 15.5 %collective-permute-start.14 = (f32[1120,128]{1,0:T(8,128)S(1)}, f32[1120,128]{1,0:T(8,128)S(1)}, u32[]{:S(2)}, u32[]{:S(2)}) collective-permute-start(f32[1120,128]{1,0:T(8,128)S(1)} %collective-permute-done.11.refs_2_), channel_id=1, source_target_pairs={{2,3},{9,8},{18,19},{25,24},{6,7},{13,12},{22,23},{29,28}} | collective-permute-start | bytes 1720328 | tf_op jit(solution)/shard_map/ppermute | solution.py:306
  103.0 26.4 %collective-permute-start.19 = (f32[528,512]{1,0:T(8,128)S(1)}, f32[528,512]{1,0:T(8,128)S(1)}, u32[]{:S(2)}, u32[]{:S(2)}) collective-permute-start(f32[528,512]{1,0:T(8,128)S(1)} %copy-done.10), channel_id=1, source_target_pairs={{0,16},{8,24},{16,0},{24,8},{1,17},{9,25},{17,1},{25,9},{2,18},{10... | collective-permute-start | bytes 3244040 | tf_op jit(solution)/shard_map/ppermute | solution.py:295
  103.6 5.8 %collective-permute-start.15 = (f32[880,128]{1,0:T(8,128)S(1)}, f32[880,128]{1,0:T(8,128)S(1)}, u32[]{:S(2)}, u32[]{:S(2)}) collective-permute-start(f32[880,128]{1,0:T(8,128)S(1)} %collective-permute-done.10.refs_1_.refs_0_), channel_id=1, source_target_pairs={{0,8},{8,0},{16,24},{24,16},{1,9},{9,1},{17,25},{25,17},{2,10},{10... | collective-permute-start | bytes 1351688 | tf_op jit(solution)/shard_map/ppermute | solution.py:295
  107.9 9.9 %collective-permute-start.13 = (f32[880,128]{1,0:T(8,128)S(1)}, f32[880,128]{1,0:T(8,128)S(1)}, u32[]{:S(2)}, u32[]{:S(2)}) collective-permute-start(f32[880,128]{1,0:T(8,128)S(1)} %collective-permute-done.10.refs_1_.refs_0_), channel_id=1, source_target_pairs={{1,2},{2,3},{9,8},{10,9},{17,18},{18,19},{25,24},{26,25},{5,6},{6,... | collective-permute-start | bytes 1351688 | tf_op jit(solution)/shard_map/ppermute | solution.py:306
  108.6 10.0 %collective-permute-start.17 = (f32[1120,128]{1,0:T(8,128)S(1)}, f32[1120,128]{1,0:T(8,128)S(1)}, u32[]{:S(2)}, u32[]{:S(2)}) collective-permute-start(f32[1120,128]{1,0:T(8,128)S(1)} %collective-permute-done.11.refs_2_), channel_id=1, source_target_pairs={{0,8},{8,0},{16,24},{24,16},{1,9},{9,1},{17,25},{25,17},{2,10},{10... | collective-permute-start | bytes 1720328 | tf_op jit(solution)/shard_map/ppermute | solution.py:295
  117.8 2.0 %collective-permute-start.18 = (f32[1120,128]{1,0:T(8,128)S(1)}, f32[1120,128]{1,0:T(8,128)S(1)}, u32[]{:S(2)}, u32[]{:S(2)}) collective-permute-start(f32[1120,128]{1,0:T(8,128)S(1)} %collective-permute-done.14.refs_4_), channel_id=1, source_target_pairs={{0,8},{8,0},{16,24},{24,16},{1,9},{9,1},{17,25},{25,17},{2,10},{10... | collective-permute-start | bytes 1720328 | tf_op jit(solution)/shard_map/ppermute | solution.py:295
  117.9 11.5 %collective-permute-start.16 = (f32[880,128]{1,0:T(8,128)S(1)}, f32[880,128]{1,0:T(8,128)S(1)}, u32[]{:S(2)}, u32[]{:S(2)}) collective-permute-start(f32[880,128]{1,0:T(8,128)S(1)} %collective-permute-done.13.refs_2_), channel_id=1, source_target_pairs={{2,3},{9,8},{18,19},{25,24},{6,7},{13,12},{22,23},{29,28}} | collective-permute-start | bytes 1351688 | tf_op jit(solution)/shard_map/ppermute | solution.py:306
  129.6 12.4 %collective-permute-start.22 = (f32[528,512]{1,0:T(8,128)S(1)}, f32[528,512]{1,0:T(8,128)S(1)}, u32[]{:S(2)}, u32[]{:S(2)}) collective-permute-start(f32[528,512]{1,0:T(8,128)S(1)} %add.59.refs_0_), channel_id=1, source_target_pairs={{0,8},{8,0},{16,24},{24,16},{1,9},{9,1},{17,25},{25,17},{2,10},{10... | collective-permute-start | bytes 3244040 | tf_op jit(solution)/shard_map/ppermute | solution.py:295
  130.1 3.0 %collective-permute-start.20 = (f32[880,128]{1,0:T(8,128)S(1)}, f32[880,128]{1,0:T(8,128)S(1)}, u32[]{:S(2)}, u32[]{:S(2)}) collective-permute-start(f32[880,128]{1,0:T(8,128)S(1)} %collective-permute-done.13.refs_2_), channel_id=1, source_target_pairs={{0,8},{8,0},{16,24},{24,16},{1,9},{9,1},{17,25},{25,17},{2,10},{10... | collective-permute-start | bytes 1351688 | tf_op jit(solution)/shard_map/ppermute | solution.py:295
  130.2 3.5 %collective-permute-start.21 = (f32[880,128]{1,0:T(8,128)S(1)}, f32[880,128]{1,0:T(8,128)S(1)}, u32[]{:S(2)}, u32[]{:S(2)}) collective-permute-start(f32[880,128]{1,0:T(8,128)S(1)} %collective-permute-done.16.refs_4_), channel_id=1, source_target_pairs={{0,8},{8,0},{16,24},{24,16},{1,9},{9,1},{17,25},{25,17},{2,10},{10... | collective-permute-start | bytes 1351688 | tf_op jit(solution)/shard_map/ppermute | solution.py:295
  (21 other events, 114.5 us)

commit v4 on v3

--- a/solution.py
+++ b/solution.py
@@ -467,8 +467,8 @@
     layer_sum(0)
     far_sum(0)
     spread(0)
+    finish(0, own, 2, whole_block[0])
     far_send(1)
-    finish(0, own, 2, whole_block[0])
     layer_finish(0)
     step(0, 0)
     far_sum(1)

time: 150 us -> 145 us (0.967)
  waiting for transfers between devices: 31.1 us -> 26 us
    all_to_all x2, waiting for transfers between devices: 17.8 us -> 12.8 us  [project_keep(): kept[c] = lax.all_to_all(chip, 'tensor', 0, 0)]
  transfers between devices with their start and end apart: 25 -> 25, of which waited for: 10 -> 10; matrix products, arithmetic and copies ran while one was open for 1% -> 1% of each run, Pallas kernels for 42% -> 43%
where the time goes in v4:
time: 145 us; the launch traced here: 144 us
  Pallas kernels  72.8 us (50%)
  starting transfers between devices  33.1 us (23%)
  waiting for transfers between devices  26 us (18%)
  local copies, waits for them, and re-layouts  9.03 us (6%)
  other arithmetic  2.16 us (1%)
    pallas_call x7, Pallas kernels, update(): pl.pallas_call(functools.partial(update_kernel, at, unit, sub, subs, dept...  45.3 us
    pallas_call x4, Pallas kernels, project(): pl.pallas_call(functools.partial(project_kernel, at, count, tile), in_spe...  19.9 us
    ppermute x17, waiting for transfers between devices, swap_groups(): return lax.ppermute(x, 'groups', [(g, g ^ bit) for g in range(4)])  13.3 us
    all_to_all x2, waiting for transfers between devices, project_keep(): kept[c] = lax.all_to_all(chip, 'tensor', 0, 0)  12.8 us
    ppermute x17, starting transfers between devices, swap_groups(): return lax.ppermute(x, 'groups', [(g, g ^ bit) for g in range(4)])  12.6 us
    ppermute x6, starting transfers between devices, shift(): return lax.ppermute(x, ('groups', 'tensor'), pairs)  10.6 us
    all_to_all x2, starting transfers between devices, project_keep(): kept[c] = lax.all_to_all(chip, 'tensor', 0, 0)  9.83 us
    unnamed x42, local copies, waits for them, and re-layouts  8.29 us
  transfers between devices with their start and end apart: 25, of which 10 were waited for; matrix products, arithmetic and copies ran while one was open for 1% of the time, Pallas kernels for 43%

profile of v4, /device:TPU:0, one launch (start us, length us, event | category | flops | bytes accessed | tf_op | source)
XLA Modules:
  0.0 144.4 jit_solution(3007363761346347427)
XLA Ops:
  2.2 5.1 %project.4 = f32[2240,128]{1,0:T(8,128)} custom-call(s32[162]{0:T(256)S(1)} %bitcast.23, f32[16000,256]{1,0:T(8,128)} %refs_7_.3, bf16[16000,256]{1,0:T(8,128)(2,1)} %bitcast.36, f32[64,256]{1,0:T(8,128)S(1)} %bitcast.14), custom_call_target="tpu_custom_call" | custom-call | tf_op jit(solution)/shard_map/project/pallas_call | solution.py:98
  7.8 3.3 %widen.2 = f32[1056,512]{1,0:T(8,128)} custom-call(s32[162]{0:T(256)S(1)} %bitcast.24, bf16[2112,512]{1,0:T(8,128)(2,1)} %bitcast.44), custom_call_target="tpu_custom_call" | custom-call | tf_op jit(solution)/shard_map/widen/pallas_call | solution.py:268
  12.3 5.8 %project.5 = f32[2240,128]{1,0:T(8,128)} custom-call(s32[162]{0:T(256)S(1)} %bitcast.25, f32[16000,256]{1,0:T(8,128)} %refs_7_.3, bf16[16000,256]{1,0:T(8,128)(2,1)} %bitcast.37, f32[64,256]{1,0:T(8,128)S(1)} %bitcast.15, f32[2240,128]{1,0:T(8,128)} %copy-done.8), custom_call_target="tpu_custom_call" | custom-call | tf_op jit(solution)/shard_map/project/pallas_call | solution.py:98
  18.1 6.3 %all-to-all-start.1 = ((f32[4,560,128]{2,1,0:T(8,128)}), f32[4,560,128]{2,1,0:T(8,128)S(1)}, u32[]{:S(2)}, u32[]{:S(2)}) async-start(f32[4,560,128]{2,1,0:T(8,128)} %bitcast.46), calls=%async_computation.1 | async-start | bytes 2293760 | tf_op jit(solution)/shard_map/all_to_all | solution.py:428
  24.4 3.7 %project.6 = f32[1760,128]{1,0:T(8,128)S(1)} custom-call(s32[162]{0:T(256)S(1)} %bitcast.26, f32[16000,256]{1,0:T(8,128)} %refs_7_.3, bf16[16000,256]{1,0:T(8,128)(2,1)} %bitcast.38, f32[64,256]{1,0:T(8,128)S(1)} %bitcast.16), custom_call_target="tpu_custom_call" | custom-call | tf_op jit(solution)/shard_map/project/pallas_call | solution.py:98
  29.5 4.3 %widen.3 = (f32[528,512]{1,0:T(8,128)}, f32[528,512]{1,0:T(8,128)}) custom-call(s32[162]{0:T(256)S(1)} %bitcast.27, bf16[2112,512]{1,0:T(8,128)(2,1)} %bitcast.45, f32[1056,512]{1,0:T(8,128)} %copy-done.7), custom_call_target="tpu_custom_call" | custom-call | tf_op jit(solution)/shard_map/widen/pallas_call | solution.py:268
  36.4 5.3 %project.7 = f32[1760,128]{1,0:T(8,128)} custom-call(s32[162]{0:T(256)S(1)} %bitcast.28, f32[16000,256]{1,0:T(8,128)} %refs_7_.3, bf16[16000,256]{1,0:T(8,128)(2,1)} %bitcast.39, f32[64,256]{1,0:T(8,128)S(1)} %bitcast.17, f32[1760,128]{1,0:T(8,128)} %copy-done.11), custom_call_target="tpu_custom_call" | custom-call | tf_op jit(solution)/shard_map/project/pallas_call | solution.py:98
  41.7 10.8 %all-to-all-done.1 = f32[4,560,128]{2,1,0:T(8,128)S(1)} async-done(((f32[4,560,128]{2,1,0:T(8,128)}), f32[4,560,128]{2,1,0:T(8,128)S(1)}, u32[]{:S(2)}, u32[]{:S(2)}) %all-to-all-start.1) | async-done | bytes 1146912 | tf_op jit(solution)/shard_map/all_to_all | solution.py:428
  52.5 3.5 %all-to-all-start = ((f32[4,440,128]{2,1,0:T(8,128)}), f32[4,440,128]{2,1,0:T(8,128)S(1)}, u32[]{:S(2)}, u32[]{:S(2)}) async-start(f32[4,440,128]{2,1,0:T(8,128)} %bitcast.4), calls=%async_computation | async-start | bytes 1802240 | tf_op jit(solution)/shard_map/all_to_all | solution.py:428
  57.6 3.3 %collective-permute-done.3 = f32[528,512]{1,0:T(8,128)} collective-permute-done((f32[528,512]{1,0:T(8,128)}, f32[528,512]{1,0:T(8,128)}, u32[]{:S(2)}, u32[]{:S(2)}) %collective-permute-start.3) | collective-permute-done | bytes 1081376 | tf_op jit(solution)/shard_map/ppermute | solution.py:295
  60.9 1.8 %add.52.refs_0_ = f32[528,512]{1,0:T(8,128)S(1)} add(f32[528,512]{1,0:T(8,128)} %get-tuple-element.57, f32[528,512]{1,0:T(8,128)} %collective-permute-done.3) | non-fusion elementwise | flops 270336 | bytes 3244032 | tf_op jit(solution)/shard_map/add | solution.py:396
  62.8 3.8 %collective-permute-done.4 = f32[560,128]{1,0:T(8,128)S(1)} collective-permute-done((f32[560,128]{1,0:T(8,128)S(1)}, f32[560,128]{1,0:T(8,128)S(1)}, u32[]{:S(2)}, u32[]{:S(2)}) %collective-permute-start.4) | collective-permute-done | bytes 286752 | tf_op jit(solution)/shard_map/ppermute | solution.py:295
  68.2 4.0 %collective-permute-start.6 = (f32[1120,128]{1,0:T(8,128)S(1)}, f32[1120,128]{1,0:T(8,128)S(1)}, u32[]{:S(2)}, u32[]{:S(2)}) collective-permute-start(f32[1120,128]{1,0:T(8,128)S(1)} %constant_dynamic-update-slice_fusion.refs_0_), channel_id=1, source_target_pairs={{0,1},{1,2},{2,3},{9,8},{10,9},{11,10},{16,17},{17,18},{18,19},{25... | collective-permute-start | bytes 1720328 | tf_op jit(solution)/shard_map/ppermute | solution.py:306
  72.2 5.0 %embed_update.5 = (f32[16000,256]{1,0:T(8,128)}, f32[16000,256]{1,0:T(8,128)}) custom-call(s32[162]{0:T(256)S(1)} %bitcast.29, f32[1120,128]{1,0:T(8,128)S(1)} %constant_dynamic-update-slice_fusion.refs_0_, f32[64,256]{1,0:T(8,128)S(1)} %bitcast.18, f32[16000,256]{1,0:T(8,128)} %refs_7_.3, f32[16000,256]{1,0:T(8,128)} %refs_8_.3), custom_call_target="tpu_custom_call" | custom-call | tf_op jit(solution)/shard_map/embed_update/pallas_call | solution.py:197
  77.2 2.0 %all-to-all-done = f32[4,440,128]{2,1,0:T(8,128)S(1)} async-done(((f32[4,440,128]{2,1,0:T(8,128)}), f32[4,440,128]{2,1,0:T(8,128)S(1)}, u32[]{:S(2)}, u32[]{:S(2)}) %all-to-all-start) | async-done | bytes 901152 | tf_op jit(solution)/shard_map/all_to_all | solution.py:428
  80.8 5.6 %layer_update.2 = (f32[2112,512]{1,0:T(8,128)}, f32[2112,512]{1,0:T(8,128)}) custom-call(s32[162]{0:T(256)S(1)} %bitcast.30, f32[528,512]{1,0:T(8,128)} %copy-done.5, f32[528,512]{1,0:T(8,128)} %collective-permute-done.7.refs_1_, f32[2112,512]{1,0:T(8,128)} %bitcast.40, f32[2112,512]{1,0:T(8,128)} %bitcast.42), custom_call_target="tpu_custom_call" | custom-call | tf_op jit(solution)/shard_map/layer_update/pallas_call | solution.py:197
  88.1 3.9 %collective-permute-start.10 = (f32[880,128]{1,0:T(8,128)S(1)}, f32[880,128]{1,0:T(8,128)S(1)}, u32[]{:S(2)}, u32[]{:S(2)}) collective-permute-start(f32[880,128]{1,0:T(8,128)S(1)} %constant_dynamic-update-slice_fusion.2.refs_0_), channel_id=1, source_target_pairs={{0,1},{1,2},{2,3},{9,8},{10,9},{11,10},{16,17},{17,18},{18,19},{25... | collective-permute-start | bytes 1351688 | tf_op jit(solution)/shard_map/ppermute | solution.py:306
  92.8 5.2 %embed_update.6 = (f32[16000,256]{1,0:T(8,128)}, f32[16000,256]{1,0:T(8,128)}) custom-call(s32[162]{0:T(256)S(1)} %bitcast.31, f32[1120,128]{1,0:T(8,128)S(1)} %collective-permute-done.6.refs_0_, f32[1120,128]{1,0:T(8,128)} %copy-done.6, f32[64,256]{1,0:T(8,128)S(1)} %bitcast.19, ...), custom_call_target="tpu_custom_call", output_to_operand_aliasing={{0}: (6, {}), {1}: (7, {})} | custom-call | tf_op jit(solution)/shard_map/embed_update/pallas_call | solution.py:197
  99.5 3.4 %collective-permute-start.15 = (f32[880,128]{1,0:T(8,128)S(1)}, f32[880,128]{1,0:T(8,128)S(1)}, u32[]{:S(2)}, u32[]{:S(2)}) collective-permute-start(f32[880,128]{1,0:T(8,128)S(1)} %collective-permute-done.10.refs_1_.refs_0_), channel_id=1, source_target_pairs={{0,8},{8,0},{16,24},{24,16},{1,9},{9,1},{17,25},{25,17},{2,10},{10... | collective-permute-start | bytes 1351688 | tf_op jit(solution)/shard_map/ppermute | solution.py:295
  105.2 7.6 %embed_update.7 = (f32[16000,256]{1,0:T(8,128)}, f32[16000,256]{1,0:T(8,128)}) custom-call(s32[162]{0:T(256)S(1)} %bitcast.32, f32[880,128]{1,0:T(8,128)S(1)} %constant_dynamic-update-slice_fusion.2.refs_0_, f32[880,128]{1,0:T(8,128)S(1)} %collective-permute-done.10.refs_1_.refs_0_, ...), custom_call_target="tpu_custom_call", output_to_operand_aliasing={{0}: (7, {}), {1}: (8, {})} | custom-call | tf_op jit(solution)/shard_map/embed_update/pallas_call | solution.py:197
  115.7 8.7 %embed_update.8 = (f32[16000,256]{1,0:T(8,128)}, f32[16000,256]{1,0:T(8,128)}) custom-call(s32[162]{0:T(256)S(1)} %bitcast.33, f32[1120,128]{1,0:T(8,128)S(1)} %collective-permute-done.6.refs_0_, f32[1120,128]{1,0:T(8,128)} %copy-done.6, f32[1120,128]{1,0:T(8,128)} %copy-done.12, ...), custom_call_target="tpu_custom_call", output_to_operand_aliasing={{0}: (10, {}), {1}: (11, {})} | custom-call | tf_op jit(solution)/shard_map/embed_update/pallas_call | solution.py:197
  126.2 2.5 %collective-permute-done.20.refs_3_ = f32[880,128]{1,0:T(8,128)S(1)} collective-permute-done((f32[880,128]{1,0:T(8,128)S(1)}, f32[880,128]{1,0:T(8,128)S(1)}, u32[]{:S(2)}, u32[]{:S(2)}) %collective-permute-start.20) | collective-permute-done | bytes 450592 | tf_op jit(solution)/shard_map/ppermute | solution.py:295
  130.0 7.5 %embed_update.9 = (f32[16000,256]{1,0:T(8,128)}, f32[16000,256]{1,0:T(8,128)}) custom-call(s32[162]{0:T(256)S(1)} %bitcast.34, f32[880,128]{1,0:T(8,128)S(1)} %collective-permute-done.10.refs_1_.refs_0_, f32[880,128]{1,0:T(8,128)S(1)} %copy-done.3, f32[880,128]{1,0:T(8,128)} %copy-done.16, ...), custom_call_target="tpu_custom_call", output_to_operand_aliasing={{0}: (10, {}), {1}: (11, {})} | custom-call | tf_op jit(solution)/shard_map/embed_update/pallas_call | solution.py:197
  138.6 5.6 %layer_update.3 = (f32[2112,512]{1,0:T(8,128)}, f32[2112,512]{1,0:T(8,128)}) custom-call(s32[162]{0:T(256)S(1)} %bitcast.35, f32[528,512]{1,0:T(8,128)} %copy-done.4, f32[528,512]{1,0:T(8,128)} %copy-done.9, f32[2112,512]{1,0:T(8,128)} %bitcast.41, f32[2112,512]{1,0:T(8,128)} %bitcast.43, ...), custom_call_target="tpu_custom_call", output_to_operand_aliasing={{0}: (5, {}), {1}: (6, {})} | custom-call | tf_op jit(solution)/shard_map/layer_update/pallas_call | solution.py:197
  (90 shorter events, 25.1 us)
Async XLA Ops:
  7.3 3.9 %collective-permute-start = (f32[2240,128]{1,0:T(8,128)}, f32[2240,128]{1,0:T(8,128)S(1)}, u32[]{:S(2)}, u32[]{:S(2)}) collective-permute-start(f32[2240,128]{1,0:T(8,128)} %project.4), channel_id=1, source_target_pairs={{0,8},{8,0},{16,24},{24,16},{1,9},{9,1},{17,25},{25,17},{2,10},{10... | collective-permute-start | bytes 3440648 | tf_op jit(solution)/shard_map/ppermute | solution.py:295
  11.1 17.1 %collective-permute-start.1 = (f32[1056,512]{1,0:T(8,128)}, f32[1056,512]{1,0:T(8,128)S(1)}, u32[]{:S(2)}, u32[]{:S(2)}) collective-permute-start(f32[1056,512]{1,0:T(8,128)} %widen.2), channel_id=1, source_target_pairs={{0,8},{8,0},{16,24},{24,16},{1,9},{9,1},{17,25},{25,17},{2,10},{10... | collective-permute-start | bytes 6488072 | tf_op jit(solution)/shard_map/ppermute | solution.py:295
  18.1 34.4 %all-to-all-start.1 = ((f32[4,560,128]{2,1,0:T(8,128)}), f32[4,560,128]{2,1,0:T(8,128)S(1)}, u32[]{:S(2)}, u32[]{:S(2)}) async-start(f32[4,560,128]{2,1,0:T(8,128)} %bitcast.46), calls=%async_computation.1 | async-start | bytes 2293760 | tf_op jit(solution)/shard_map/all_to_all | solution.py:428
  28.1 7.3 %collective-permute-start.2 = (f32[1760,128]{1,0:T(8,128)S(1)}, f32[1760,128]{1,0:T(8,128)S(1)}, u32[]{:S(2)}, u32[]{:S(2)}) collective-permute-start(f32[1760,128]{1,0:T(8,128)S(1)} %project.6), channel_id=1, source_target_pairs={{0,8},{8,0},{16,24},{24,16},{1,9},{9,1},{17,25},{25,17},{2,10},{10... | collective-permute-start | bytes 2703368 | tf_op jit(solution)/shard_map/ppermute | solution.py:295
  33.9 27.0 %collective-permute-start.3 = (f32[528,512]{1,0:T(8,128)}, f32[528,512]{1,0:T(8,128)}, u32[]{:S(2)}, u32[]{:S(2)}) collective-permute-start(f32[528,512]{1,0:T(8,128)} %get-tuple-element.57), channel_id=1, source_target_pairs={{0,16},{8,24},{16,0},{24,8},{1,17},{9,25},{17,1},{25,9},{2,18},{10... | collective-permute-start | bytes 3244040 | tf_op jit(solution)/shard_map/ppermute | solution.py:295
  52.5 26.7 %all-to-all-start = ((f32[4,440,128]{2,1,0:T(8,128)}), f32[4,440,128]{2,1,0:T(8,128)S(1)}, u32[]{:S(2)}, u32[]{:S(2)}) async-start(f32[4,440,128]{2,1,0:T(8,128)} %bitcast.4), calls=%async_computation | async-start | bytes 1802240 | tf_op jit(solution)/shard_map/all_to_all | solution.py:428
  56.0 10.5 %collective-permute-start.4 = (f32[560,128]{1,0:T(8,128)S(1)}, f32[560,128]{1,0:T(8,128)S(1)}, u32[]{:S(2)}, u32[]{:S(2)}) collective-permute-start(f32[560,128]{1,0:T(8,128)S(1)} %add_bitcast_fusion), channel_id=1, source_target_pairs={{0,16},{8,24},{16,0},{24,8},{1,17},{9,25},{17,1},{25,9},{2,18},{10... | collective-permute-start | bytes 860168 | tf_op jit(solution)/shard_map/ppermute | solution.py:295
  62.7 18.1 %collective-permute-start.7 = (f32[528,512]{1,0:T(8,128)S(1)}, f32[528,512]{1,0:T(8,128)}, u32[]{:S(2)}, u32[]{:S(2)}) collective-permute-start(f32[528,512]{1,0:T(8,128)S(1)} %add.52.refs_0_), channel_id=1, source_target_pairs={{0,8},{8,0},{16,24},{24,16},{1,9},{9,1},{17,25},{25,17},{2,10},{10... | collective-permute-start | bytes 3244040 | tf_op jit(solution)/shard_map/ppermute | solution.py:295
  66.6 1.6 %collective-permute-start.5 = (f32[560,128]{1,0:T(8,128)S(1)}, f32[560,128]{1,0:T(8,128)S(1)}, u32[]{:S(2)}, u32[]{:S(2)}) collective-permute-start(f32[560,128]{1,0:T(8,128)S(1)} %add.53), channel_id=1, source_target_pairs={{0,8},{8,0},{16,24},{24,16},{1,9},{9,1},{17,25},{25,17},{2,10},{10... | collective-permute-start | bytes 860168 | tf_op jit(solution)/shard_map/ppermute | solution.py:295
  68.2 18.2 %collective-permute-start.6 = (f32[1120,128]{1,0:T(8,128)S(1)}, f32[1120,128]{1,0:T(8,128)S(1)}, u32[]{:S(2)}, u32[]{:S(2)}) collective-permute-start(f32[1120,128]{1,0:T(8,128)S(1)} %constant_dynamic-update-slice_fusion.refs_0_), channel_id=1, source_target_pairs={{0,1},{1,2},{2,3},{9,8},{10,9},{11,10},{16,17},{17,18},{18,19},{25... | collective-permute-start | bytes 1720328 | tf_op jit(solution)/shard_map/ppermute | solution.py:306
  79.2 7.2 %collective-permute-start.8 = (f32[440,128]{1,0:T(8,128)S(1)}, f32[440,128]{1,0:T(8,128)S(1)}, u32[]{:S(2)}, u32[]{:S(2)}) collective-permute-start(f32[440,128]{1,0:T(8,128)S(1)} %add_bitcast_fusion.1), channel_id=1, source_target_pairs={{0,16},{8,24},{16,0},{24,8},{1,17},{9,25},{17,1},{25,9},{2,18},{10... | collective-permute-start | bytes 675848 | tf_op jit(solution)/shard_map/ppermute | solution.py:295
  86.6 5.4 %collective-permute-start.12 = (f32[1120,128]{1,0:T(8,128)S(1)}, f32[1120,128]{1,0:T(8,128)S(1)}, u32[]{:S(2)}, u32[]{:S(2)}) collective-permute-start(f32[1120,128]{1,0:T(8,128)S(1)} %collective-permute-done.6.refs_0_), channel_id=1, source_target_pairs={{0,8},{8,0},{16,24},{24,16},{1,9},{9,1},{17,25},{25,17},{2,10},{10... | collective-permute-start | bytes 1720328 | tf_op jit(solution)/shard_map/ppermute | solution.py:295
  87.1 10.9 %collective-permute-start.11 = (f32[1120,128]{1,0:T(8,128)S(1)}, f32[1120,128]{1,0:T(8,128)S(1)}, u32[]{:S(2)}, u32[]{:S(2)}) collective-permute-start(f32[1120,128]{1,0:T(8,128)S(1)} %collective-permute-done.6.refs_0_), channel_id=1, source_target_pairs={{1,2},{2,3},{9,8},{10,9},{17,18},{18,19},{25,24},{26,25},{5,6},{6,... | collective-permute-start | bytes 1720328 | tf_op jit(solution)/shard_map/ppermute | solution.py:306
  88.1 10.7 %collective-permute-start.10 = (f32[880,128]{1,0:T(8,128)S(1)}, f32[880,128]{1,0:T(8,128)S(1)}, u32[]{:S(2)}, u32[]{:S(2)}) collective-permute-start(f32[880,128]{1,0:T(8,128)S(1)} %constant_dynamic-update-slice_fusion.2.refs_0_), channel_id=1, source_target_pairs={{0,1},{1,2},{2,3},{9,8},{10,9},{11,10},{16,17},{17,18},{18,19},{25... | collective-permute-start | bytes 1351688 | tf_op jit(solution)/shard_map/ppermute | solution.py:306
  98.0 14.8 %collective-permute-start.14 = (f32[1120,128]{1,0:T(8,128)S(1)}, f32[1120,128]{1,0:T(8,128)S(1)}, u32[]{:S(2)}, u32[]{:S(2)}) collective-permute-start(f32[1120,128]{1,0:T(8,128)S(1)} %collective-permute-done.11.refs_2_), channel_id=1, source_target_pairs={{2,3},{9,8},{18,19},{25,24},{6,7},{13,12},{22,23},{29,28}} | collective-permute-start | bytes 1720328 | tf_op jit(solution)/shard_map/ppermute | solution.py:306
  98.7 25.7 %collective-permute-start.19 = (f32[528,512]{1,0:T(8,128)S(1)}, f32[528,512]{1,0:T(8,128)S(1)}, u32[]{:S(2)}, u32[]{:S(2)}) collective-permute-start(f32[528,512]{1,0:T(8,128)S(1)} %copy-done.10), channel_id=1, source_target_pairs={{0,16},{8,24},{16,0},{24,8},{1,17},{9,25},{17,1},{25,9},{2,18},{10... | collective-permute-start | bytes 3244040 | tf_op jit(solution)/shard_map/ppermute | solution.py:295
  99.5 4.9 %collective-permute-start.15 = (f32[880,128]{1,0:T(8,128)S(1)}, f32[880,128]{1,0:T(8,128)S(1)}, u32[]{:S(2)}, u32[]{:S(2)}) collective-permute-start(f32[880,128]{1,0:T(8,128)S(1)} %collective-permute-done.10.refs_1_.refs_0_), channel_id=1, source_target_pairs={{0,8},{8,0},{16,24},{24,16},{1,9},{9,1},{17,25},{25,17},{2,10},{10... | collective-permute-start | bytes 1351688 | tf_op jit(solution)/shard_map/ppermute | solution.py:295
  102.9 9.9 %collective-permute-start.13 = (f32[880,128]{1,0:T(8,128)S(1)}, f32[880,128]{1,0:T(8,128)S(1)}, u32[]{:S(2)}, u32[]{:S(2)}) collective-permute-start(f32[880,128]{1,0:T(8,128)S(1)} %collective-permute-done.10.refs_1_.refs_0_), channel_id=1, source_target_pairs={{1,2},{2,3},{9,8},{10,9},{17,18},{18,19},{25,24},{26,25},{5,6},{6,... | collective-permute-start | bytes 1351688 | tf_op jit(solution)/shard_map/ppermute | solution.py:306
  103.6 10.0 %collective-permute-start.17 = (f32[1120,128]{1,0:T(8,128)S(1)}, f32[1120,128]{1,0:T(8,128)S(1)}, u32[]{:S(2)}, u32[]{:S(2)}) collective-permute-start(f32[1120,128]{1,0:T(8,128)S(1)} %collective-permute-done.11.refs_2_), channel_id=1, source_target_pairs={{0,8},{8,0},{16,24},{24,16},{1,9},{9,1},{17,25},{25,17},{2,10},{10... | collective-permute-start | bytes 1720328 | tf_op jit(solution)/shard_map/ppermute | solution.py:295
  112.8 2.0 %collective-permute-start.18 = (f32[1120,128]{1,0:T(8,128)S(1)}, f32[1120,128]{1,0:T(8,128)S(1)}, u32[]{:S(2)}, u32[]{:S(2)}) collective-permute-start(f32[1120,128]{1,0:T(8,128)S(1)} %collective-permute-done.14.refs_4_), channel_id=1, source_target_pairs={{0,8},{8,0},{16,24},{24,16},{1,9},{9,1},{17,25},{25,17},{2,10},{10... | collective-permute-start | bytes 1720328 | tf_op jit(solution)/shard_map/ppermute | solution.py:295
  112.9 11.5 %collective-permute-start.16 = (f32[880,128]{1,0:T(8,128)S(1)}, f32[880,128]{1,0:T(8,128)S(1)}, u32[]{:S(2)}, u32[]{:S(2)}) collective-permute-start(f32[880,128]{1,0:T(8,128)S(1)} %collective-permute-done.13.refs_2_), channel_id=1, source_target_pairs={{2,3},{9,8},{18,19},{25,24},{6,7},{13,12},{22,23},{29,28}} | collective-permute-start | bytes 1351688 | tf_op jit(solution)/shard_map/ppermute | solution.py:306
  124.7 12.9 %collective-permute-start.22 = (f32[528,512]{1,0:T(8,128)S(1)}, f32[528,512]{1,0:T(8,128)S(1)}, u32[]{:S(2)}, u32[]{:S(2)}) collective-permute-start(f32[528,512]{1,0:T(8,128)S(1)} %add.59.refs_0_), channel_id=1, source_target_pairs={{0,8},{8,0},{16,24},{24,16},{1,9},{9,1},{17,25},{25,17},{2,10},{10... | collective-permute-start | bytes 3244040 | tf_op jit(solution)/shard_map/ppermute | solution.py:295
  125.7 3.0 %collective-permute-start.20 = (f32[880,128]{1,0:T(8,128)S(1)}, f32[880,128]{1,0:T(8,128)S(1)}, u32[]{:S(2)}, u32[]{:S(2)}) collective-permute-start(f32[880,128]{1,0:T(8,128)S(1)} %collective-permute-done.13.refs_2_), channel_id=1, source_target_pairs={{0,8},{8,0},{16,24},{24,16},{1,9},{9,1},{17,25},{25,17},{2,10},{10... | collective-permute-start | bytes 1351688 | tf_op jit(solution)/shard_map/ppermute | solution.py:295
  125.7 3.5 %collective-permute-start.21 = (f32[880,128]{1,0:T(8,128)S(1)}, f32[880,128]{1,0:T(8,128)S(1)}, u32[]{:S(2)}, u32[]{:S(2)}) collective-permute-start(f32[880,128]{1,0:T(8,128)S(1)} %collective-permute-done.16.refs_4_), channel_id=1, source_target_pairs={{0,8},{8,0},{16,24},{24,16},{1,9},{9,1},{17,25},{25,17},{2,10},{10... | collective-permute-start | bytes 1351688 | tf_op jit(solution)/shard_map/ppermute | solution.py:295
  (21 other events, 107.4 us)
